TPU v7x, 256 devices: a whole 4x4x8 slice. The times are simulated.
256 devices in a mesh: len: 32 (over z_lo, y, core), wid: 8 (over x, z_hi).
Axes of the slice: x: 4, y: 4, z: 8 (z_hi: 2, z_lo: 4; z = z_hi * 4 + z_lo), core: 2. Of those that a mesh axis runs over, the one named last changes fastest.
Arguments:
- conserved: float32 [9, 6, 6, 6, 32, 1024], P(None, None, None, None, 'len', 'wid'), may hold values from -1.3 to 12.5, as said below
- ends_kind: int32 [2, 32, 32], P(None, 'wid'), may hold values from 0 to 2
- sides_kind: int32 [2, 32, 32], P(None, 'len'), may hold values from 0 to 2
- walls_kind: int32 [2, 32, 32], P(None, 'len', 'wid'), may hold values from 0 to 2
Outputs:
- updated: float32 [9, 6, 6, 6, 32, 1024], P(None, None, None, None, 'len', 'wid')
- time_step: float32 [], replicated
Inputs may be any that keep to these rules, and one draw needn't show every extreme that they name: `conserved`: density and pressure of every node lie between 0.7 and 1.4. `ends_kind`: 0 marks an inflow port of the nozzle, 1 a wall, 2 the free surface. `sides_kind`: 0 marks an inflow port of the nozzle, 1 a wall, 2 the free surface. `walls_kind`: 0 marks an inflow port of the nozzle, 1 a wall, 2 the free surface.
All inputs are finite; a program needn't handle non-finite values.
Results may differ from a plain program's by a relative error of at most 0.00012.
Values sent between devices are 32-bit elements; how exact they have to be, the bound alone decides.
A program may use at most 128 MiB of HBM per device.

v0:
```python
import jax
import jax.numpy as jnp
import numpy as np
from jax import lax
from jax.sharding import PartitionSpec as P

EZ = 32


GAMMA = 5.0 / 3.0
GLM_SPEED = 2.0
JET_SPEED = 0.8
BRAKE_FIELD = 1.0
CFL_NUMBER = 0.1
END_WEIGHT = 1.0 / 15.0
JACOBIAN_INV = 2.0


def shifted(array, axis, by):
    count = lax.axis_size(axis)
    pairs = [(i, i + by) for i in range(count) if 0 <= i + by < count]
    return lax.ppermute(array, axis, pairs)


def lgl_derivative():
    points = np.array(
        [
            -1.0,
            -0.7650553239294647,
            -0.2852315164806451,
            0.2852315164806451,
            0.7650553239294647,
            1.0,
        ]
    )
    node_count = points.shape[0]
    barycentric = np.ones(node_count)
    for row_index in range(node_count):
        for column in range(node_count):
            if row_index != column:
                barycentric[row_index] = barycentric[row_index] / (
                    points[row_index] - points[column]
                )
    matrix = np.zeros((node_count, node_count))
    for row_index in range(node_count):
        for column in range(node_count):
            if row_index != column:
                matrix[row_index, column] = (
                    barycentric[column]
                    / barycentric[row_index]
                    / (points[row_index] - points[column])
                )
    for row_index in range(node_count):
        matrix[row_index, row_index] = -np.sum(matrix[row_index])
    return matrix.astype(np.float32)


def primitives(conserved):
    density = conserved[0]
    velocity = [conserved[1] / density, conserved[2] / density, conserved[3] / density]
    magnetic_field = [conserved[5], conserved[6], conserved[7]]
    cleaning = conserved[8]
    kinetic = 0.5 * (
        conserved[1] * velocity[0] + conserved[2] * velocity[1] + conserved[3] * velocity[2]
    )
    magnetic = 0.5 * (magnetic_field[0] ** 2 + magnetic_field[1] ** 2 + magnetic_field[2] ** 2)
    pressure = (GAMMA - 1.0) * (conserved[4] - kinetic - magnetic - 0.5 * cleaning * cleaning)
    return (density, velocity, magnetic_field, cleaning, pressure, magnetic)


def directional_flux(conserved, direction):
    density, velocity, magnetic_field, cleaning, pressure, magnetic = primitives(conserved)
    total_pressure = pressure + magnetic
    normal_velocity = velocity[direction]
    normal_field = magnetic_field[direction]
    velocity_dot_field = (
        velocity[0] * magnetic_field[0]
        + velocity[1] * magnetic_field[1]
        + velocity[2] * magnetic_field[2]
    )
    entries = [conserved[1 + direction]]
    for component in range(3):
        momentum = (
            conserved[1 + component] * normal_velocity - magnetic_field[component] * normal_field
        )
        if component == direction:
            momentum = momentum + total_pressure
        entries.append(momentum)
    entries.append(
        normal_velocity * (conserved[4] + total_pressure)
        - normal_field * velocity_dot_field
        + GLM_SPEED * cleaning * normal_field
    )
    for component in range(3):
        if component == direction:
            entries.append(GLM_SPEED * cleaning)
        else:
            entries.append(
                normal_velocity * magnetic_field[component] - normal_field * velocity[component]
            )
    entries.append(GLM_SPEED * normal_field)
    return jnp.stack(entries)


def wave_speed(conserved, direction):
    density, velocity, magnetic_field, cleaning, pressure, magnetic = primitives(conserved)
    acoustic_speed_sq = GAMMA * pressure / density
    along_sq = magnetic_field[direction] ** 2 / density
    transverse_axis = (
        magnetic_field[(direction + 1) % 3] ** 2 + magnetic_field[(direction + 2) % 3] ** 2
    )
    transverse_axis = transverse_axis / density
    alfven_speed_sq = along_sq + transverse_axis
    quadratic_discrim = (
        acoustic_speed_sq - alfven_speed_sq
    ) ** 2 + 4.0 * acoustic_speed_sq * transverse_axis
    fast_magnetosonic = jnp.sqrt(
        0.5 * (acoustic_speed_sq + alfven_speed_sq + jnp.sqrt(quadratic_discrim))
    )
    return jnp.maximum(jnp.abs(velocity[direction]) + fast_magnetosonic, GLM_SPEED)


def boundary_state(interior, kind_values, direction, outward):
    inflow_values = [
        1.0,
        0.0,
        0.0,
        0.0,
        1.0 / (GAMMA - 1.0) + 0.5 * JET_SPEED**2 + 0.5 * BRAKE_FIELD**2,
        0.0,
        0.0,
        BRAKE_FIELD,
        0.0,
    ]
    inflow_values[1 + direction] = -outward * JET_SPEED
    inflow = (
        jnp.asarray(np.array(inflow_values, dtype=np.float32))
        .astype(interior.dtype)
        .reshape((9, 1, 1, 1))
    )
    mirror_values = np.ones(9, dtype=np.float32)
    mirror_values[1 + direction] = -1.0
    mirror = jnp.asarray(mirror_values).astype(interior.dtype).reshape((9, 1, 1, 1))
    wall_state = interior * mirror
    return jnp.where(kind_values == 0, inflow, jnp.where(kind_values == 1, wall_state, interior))


def triplet(ghost_state, direction):
    return (
        ghost_state,
        directional_flux(ghost_state, direction),
        wave_speed(ghost_state, direction)[None],
    )


def local_lax_friedrichs(left_state, left_flux, left_speed, right_state, right_flux, right_speed):
    return 0.5 * (left_flux + right_flux) - 0.5 * jnp.maximum(left_speed, right_speed) * (
        right_state - left_state
    )


def element_kinds(face_kinds, direction, side, elem_len, elem_wid):
    if direction == 0:
        return jnp.tile(face_kinds[0][side].reshape(elem_wid * EZ), elem_len)
    if direction == 1:
        plane = face_kinds[1][side]
        return jnp.broadcast_to(plane[:, None, :], (elem_len, elem_wid, EZ)).reshape(
            elem_len * elem_wid * EZ
        )
    return jnp.repeat(face_kinds[2][side].reshape(elem_len * elem_wid), EZ)


def width_layer(face_array, elem_len, elem_wid, index):
    lead = face_array.shape[:-1]
    return face_array.reshape(lead + (elem_len, elem_wid, EZ))[..., :, index, :]


def spread_width(piece, elem_len, elem_wid):
    lead = piece.shape[:-2]
    full = jnp.broadcast_to(piece[..., :, None, :], lead + (elem_len, elem_wid, EZ))
    return full.reshape(lead + (elem_len * elem_wid * EZ,))


def spread_length(piece, elem_len):
    return jnp.tile(piece, (1,) * (piece.ndim - 1) + (elem_len,))


def finish_ghost(received, outer_ghost, at_edge, direction):
    return triplet(jnp.where(at_edge, outer_ghost, received), direction)


def across_length(first_low, last_high):
    from_below = shifted(last_high, "len", 1)
    from_above = shifted(first_low, "len", -1)
    return (from_below, from_above)


def across_width(first_low, last_high):
    from_below = shifted(last_high, "wid", 1)
    from_above = shifted(first_low, "wid", -1)
    return (from_below, from_above)


def operator(conserved, derivative, face_kinds):
    shape = conserved.shape
    elem_len = shape[4]
    cross = shape[5]
    elem_wid = cross // EZ
    count = elem_len * cross
    flat = conserved.reshape((9, 6, 6, 6, count))
    precise = lax.Precision.HIGHEST
    fluxes = [directional_flux(flat, direction) for direction in range(3)]
    accumulated = jnp.einsum("ai,vijke->vajke", derivative, fluxes[0], precision=precise)
    accumulated = accumulated + jnp.einsum(
        "aj,vijke->viake", derivative, fluxes[1], precision=precise
    )
    accumulated = accumulated + jnp.einsum(
        "ak,vijke->vijae", derivative, fluxes[2], precision=precise
    )
    element = lax.iota(jnp.int32, count)
    position = [element // cross, element // EZ % elem_wid, element % EZ]
    extent = [elem_len, elem_wid, EZ]
    stride = [cross, EZ, 1]
    for direction in range(3):
        low_index = (slice(None),) * (1 + direction) + (0,)
        high_index = (slice(None),) * (1 + direction) + (5,)
        low_state = flat[low_index]
        high_state = flat[high_index]
        low_flux = fluxes[direction][low_index]
        high_flux = fluxes[direction][high_index]
        low_speed = wave_speed(low_state, direction)[None]
        high_speed = wave_speed(high_state, direction)[None]
        outer_low = boundary_state(
            low_state, element_kinds(face_kinds, direction, 0, elem_len, elem_wid), direction, -1.0
        )
        outer_high = boundary_state(
            high_state, element_kinds(face_kinds, direction, 1, elem_len, elem_wid), direction, 1.0
        )
        if direction == 0:
            first_packet = low_state
            last_packet = high_state
            from_below, from_above = across_length(first_packet, last_packet)
            ghost_low = finish_ghost(
                spread_length(from_below, elem_len),
                outer_low,
                lax.axis_index("len") == 0,
                direction,
            )
            ghost_high = finish_ghost(
                spread_length(from_above, elem_len),
                outer_high,
                lax.axis_index("len") == lax.axis_size("len") - 1,
                direction,
            )
        elif direction == 1:
            first_packet = width_layer(low_state, elem_len, elem_wid, 0)
            last_packet = width_layer(high_state, elem_len, elem_wid, elem_wid - 1)
            from_below, from_above = across_width(first_packet, last_packet)
            ghost_low = finish_ghost(
                spread_width(from_below, elem_len, elem_wid),
                outer_low,
                lax.axis_index("wid") == 0,
                direction,
            )
            ghost_high = finish_ghost(
                spread_width(from_above, elem_len, elem_wid),
                outer_high,
                lax.axis_index("wid") == lax.axis_size("wid") - 1,
                direction,
            )
        else:
            ghost_low = triplet(outer_low, direction)
            ghost_high = triplet(outer_high, direction)
        low_edge = position[direction] == 0
        high_edge = position[direction] == extent[direction] - 1
        left = [
            jnp.where(low_edge, ghost, jnp.roll(inner, stride[direction], axis=-1))
            for ghost, inner in zip(ghost_low, (high_state, high_flux, high_speed))
        ]
        right = [
            jnp.where(high_edge, ghost, jnp.roll(inner, -stride[direction], axis=-1))
            for ghost, inner in zip(ghost_high, (low_state, low_flux, low_speed))
        ]
        interface_low = local_lax_friedrichs(
            left[0], left[1], left[2], low_state, low_flux, low_speed
        )
        interface_high = local_lax_friedrichs(
            high_state, high_flux, high_speed, right[0], right[1], right[2]
        )
        accumulated = accumulated.at[high_index].add((interface_high - high_flux) / END_WEIGHT)
        accumulated = accumulated.at[low_index].add((low_flux - interface_low) / END_WEIGHT)
    return (-JACOBIAN_INV * accumulated).reshape(shape)


def on_device(conserved, ends_kind, sides_kind, walls_kind):
    derivative = jnp.asarray(lgl_derivative())
    face_kinds = (ends_kind, sides_kind, walls_kind)
    local_fastest = jnp.max(
        jnp.stack([jnp.max(wave_speed(conserved, direction)) for direction in range(3)])
    )
    fastest = lax.pmax(local_fastest, ("len", "wid"))
    time_step = CFL_NUMBER / (11.0 * fastest)
    first_section = conserved + time_step * operator(conserved, derivative, face_kinds)
    second_section = 0.75 * conserved + 0.25 * (
        first_section + time_step * operator(first_section, derivative, face_kinds)
    )
    updated = conserved / 3.0 + 2.0 / 3.0 * (
        second_section + time_step * operator(second_section, derivative, face_kinds)
    )
    return (updated, time_step)


def solution(mesh):
    return jax.shard_map(
        on_device,
        mesh=mesh,
        in_specs=(
            P(None, None, None, None, "len", "wid"),
            P(None, "wid", None),
            P(None, "len", None),
            P(None, "len", "wid"),
        ),
        out_specs=(P(None, None, None, None, "len", "wid"), P()),
        check_vma=False,
    )
```

profile of v0, /device:TPU:27, one launch (start us, length us, event | category | flops | bytes accessed | tf_op | source)
XLA Modules:
  0.0 453.5 jit_solution(16260795130070542969)
XLA Ops:
  3.0 3.8 collective-permute-start.1
  6.8 1.9 collective-permute-start
  11.2 7.9 %collective-permute-start.3 = (f32[9,6,6,1,32]{4,3,2,1,0:T(1,128)}, f32[9,6,6,1,32]{4,3,2,1,0:T(1,128)}, u32[]{:S(2)}, u32[]{:S(2)}) collective-permute-start(f32[9,6,6,1,32]{4,3,2,1,0:T(1,128)} %slice_bitcast_fusion.46), channel_id=1, source_target_pairs={{0,1},{1,2},{2,3},{3,4},{4,5},{5,6},{6,7},{8,9},{9,10},{10,11},{11... | collective-permute-start | bytes 124424 | tf_op jit(solution)/shard_map/ppermute | solution.py:22
  21.3 2.5 collective-permute-start.2
  34.7 2.3 fusion.623
  37.2 2.3 fusion.18
  64.7 1.9 fusion.23
  75.9 5.1 %fusion.1 = f32[9,6,6,6,128]{4,2,3,0,1:T(8,128)} fusion(f32[6,6,1,1,1]{1,0,4,2,3:T(8,128)S(1)} %copy-done.298, f32[9,6,6,128,6]{3,4,2,1,0:T(8,128)} %fusion.18, f32[9,6,6,6,128]{4,1,3,0,2:T(8,128)} %copy-done.15, f32[9,6,6,128,6]{3,4,2,1,0:T(8,128)} %fusion.623), kind=kOutput, calls=%fused_computation.7 | convolution fusion | flops 18413568 | bytes 3981456 | tf_op jit(solution)/shard_map/aj,vijke->viake/dot_general | solution.py:214
  81.1 78.5 %pmax.7 = f32[]{:T(128)} all-reduce(f32[]{:T(128)S(6)} %reduce_max.41), channel_id=1, replica_groups=mesh['len'=32,'wid'=8] {'len','wid'}, use_global_device_ids=true, to_apply=%region_3.0 | all-reduce | flops 1 | bytes 8 | tf_op jit(solution)/shard_map/pmax | solution.py:301
  188.4 1.9 fusion.109
  199.3 4.9 %scatter-add.66 = f32[9,6,6,6,128]{4,3,2,0,1:T(8,128)} dynamic-update-slice(f32[9,6,6,6,128]{4,3,2,0,1:T(8,128)} %copy_dynamic-update-slice_fusion, f32[9,6,6,1,128]{4,3,2,0,1:T(1,128)S(1)} %copy.23753, s32[]{:T(128)} %constant.580.clone.1, s32[]{:T(128)} %constant.580.clone.1, s32[]{:T(128)} %constant.580.clone.1, s32[]{:T(128)} %constant.589.clone.1, s32[]{:T(128)} %constant.580.clone.1) | dynamic-update-slice | bytes 331780 | tf_op jit(solution)/shard_map/scatter-add | solution.py:290
  204.2 2.6 slice_add_fusion.8
  206.8 5.0 %scatter-add.69 = f32[9,6,6,6,128]{4,3,2,0,1:T(8,128)} dynamic-update-slice(f32[9,6,6,6,128]{4,3,2,0,1:T(8,128)} %scatter-add.66, f32[9,6,6,1,128]{4,3,2,0,1:T(1,128)S(1)} %slice_add_fusion.8, s32[]{:T(128)} %constant.580.clone.1, s32[]{:T(128)} %constant.580.clone.1, s32[]{:T(128)} %constant.580.clone.1, s32[]{:T(128)} %constant.580.clone.1, s32[]{:T(128)} %constant.580.clone.1) | dynamic-update-slice | bytes 331780 | tf_op jit(solution)/shard_map/scatter-add | solution.py:291
  217.0 2.6 fusion.16
  220.6 2.3 fusion.14
  234.6 3.5 collective-permute-start.5
  238.8 1.9 collective-permute-start.4
  240.8 2.1 reshape_squeeze.27
  242.8 1.9 slice_bitcast_fusion.44
  244.8 5.2 %collective-permute-start.7 = (f32[9,6,6,1,32]{4,3,2,1,0:T(1,128)}, f32[9,6,6,1,32]{4,3,2,1,0:T(1,128)}, u32[]{:S(2)}, u32[]{:S(2)}) collective-permute-start(f32[9,6,6,1,32]{4,3,2,1,0:T(1,128)} %slice_bitcast_fusion.44), channel_id=1, source_target_pairs={{0,1},{1,2},{2,3},{3,4},{4,5},{5,6},{6,7},{8,9},{9,10},{10,11},{11... | collective-permute-start | bytes 124424 | tf_op jit(solution)/shard_map/ppermute | solution.py:22
  252.2 1.9 slice_bitcast_fusion.45
  254.1 5.3 %collective-permute-start.6 = (f32[9,6,6,1,32]{4,3,2,1,0:T(1,128)}, f32[9,6,6,1,32]{4,3,2,1,0:T(1,128)}, u32[]{:S(2)}, u32[]{:S(2)}) collective-permute-start(f32[9,6,6,1,32]{4,3,2,1,0:T(1,128)} %slice_bitcast_fusion.45), channel_id=1, source_target_pairs={{1,0},{2,1},{3,2},{4,3},{5,4},{6,5},{7,6},{9,8},{10,9},{11,10},{12... | collective-permute-start | bytes 124424 | tf_op jit(solution)/shard_map/ppermute | solution.py:22
  272.7 2.5 fusion.44
  277.9 2.9 fusion.2
  308.1 3.7 copy_add_fusion.7
  311.8 4.8 %scatter-add.75 = f32[9,6,6,6,128]{4,2,1,0,3:T(8,128)} dynamic-update-slice(f32[9,6,6,6,128]{4,2,1,0,3:T(8,128)} %copy.24032, f32[9,6,1,6,128]{4,2,1,0,3:T(1,128)} %copy_add_fusion.7, s32[]{:T(128)} %constant.580.clone.1, s32[]{:T(128)} %constant.580.clone.1, s32[]{:T(128)} %constant.580.clone.1, s32[]{:T(128)} %constant.580.clone.1, s32[]{:T(128)} %constant.580.clone.1) | dynamic-update-slice | bytes 331780 | tf_op jit(solution)/shard_map/scatter-add | solution.py:291
  316.7 2.3 fusion.40
  318.9 2.8 copy.24075
  322.9 4.9 %scatter-add.79 = f32[9,6,6,6,128]{4,3,2,0,1:T(8,128)} dynamic-update-slice(f32[9,6,6,6,128]{4,3,2,0,1:T(8,128)} %copy.24075, f32[9,6,6,1,128]{4,3,2,0,1:T(1,128)S(1)} %copy_add_fusion.6, s32[]{:T(128)} %constant.580.clone.1, s32[]{:T(128)} %constant.580.clone.1, s32[]{:T(128)} %constant.580.clone.1, s32[]{:T(128)} %constant.580.clone.1, s32[]{:T(128)} %constant.580.clone.1) | dynamic-update-slice | bytes 331780 | tf_op jit(solution)/shard_map/scatter-add | solution.py:291
  348.5 2.6 fusion.11
  351.1 6.3 %collective-permute-start.9 = (f32[9,6,6,128]{3,2,1,0:T(8,128)}, f32[9,6,6,128]{3,2,1,0:T(8,128)}, u32[]{:S(2)}, u32[]{:S(2)}) collective-permute-start(f32[9,6,6,128]{3,2,1,0:T(8,128)} %get-tuple-element.462), channel_id=1, source_target_pairs={{0,8},{8,16},{16,24},{24,32},{32,40},{40,48},{48,56},{56,64},{64,7... | collective-permute-start | bytes 497672 | tf_op jit(solution)/shard_map/ppermute | solution.py:22
  357.4 1.9 collective-permute-start.8
  359.4 2.1 reshape_squeeze.29
  361.4 1.9 slice_bitcast_fusion.42
  363.4 4.3 collective-permute-start.11
  369.4 2.1 reshape_squeeze.28
  371.5 1.9 slice_bitcast_fusion.43
  373.3 6.0 %collective-permute-start.10 = (f32[9,6,6,1,32]{4,3,2,1,0:T(1,128)}, f32[9,6,6,1,32]{4,3,2,1,0:T(1,128)}, u32[]{:S(2)}, u32[]{:S(2)}) collective-permute-start(f32[9,6,6,1,32]{4,3,2,1,0:T(1,128)} %slice_bitcast_fusion.43), channel_id=1, source_target_pairs={{1,0},{2,1},{3,2},{4,3},{5,4},{6,5},{7,6},{9,8},{10,9},{11,10},{12... | collective-permute-start | bytes 124424 | tf_op jit(solution)/shard_map/ppermute | solution.py:22
  391.0 1.7 slice_bitcast_fusion.3
  396.5 4.3 fusion.4
  402.2 2.2 fusion.124
  421.5 4.9 %scatter-add.84 = f32[9,6,6,6,128]{4,2,1,0,3:T(8,128)} dynamic-update-slice(f32[9,6,6,6,128]{4,2,1,0,3:T(8,128)} %copy.24244, f32[9,6,1,6,128]{4,2,1,0,3:T(1,128)S(1)} %fusion.175, s32[]{:T(128)} %constant.580.clone.1, s32[]{:T(128)} %constant.580.clone.1, s32[]{:T(128)} %constant.589.clone.1, s32[]{:T(128)} %constant.580.clone.1, s32[]{:T(128)} %constant.580.clone.1) | dynamic-update-slice | bytes 331780 | tf_op jit(solution)/shard_map/scatter-add | solution.py:290
  427.9 4.9 %scatter-add.85 = f32[9,6,6,6,128]{4,2,1,0,3:T(8,128)} dynamic-update-slice(f32[9,6,6,6,128]{4,2,1,0,3:T(8,128)} %scatter-add.84, f32[9,6,1,6,128]{4,2,1,0,3:T(1,128)S(1)} %slice_add_fusion.7, s32[]{:T(128)} %constant.580.clone.1, s32[]{:T(128)} %constant.580.clone.1, s32[]{:T(128)} %constant.580.clone.1, s32[]{:T(128)} %constant.580.clone.1, s32[]{:T(128)} %constant.580.clone.1) | dynamic-update-slice | bytes 331780 | tf_op jit(solution)/shard_map/scatter-add | solution.py:291
  432.8 2.8 copy.24329
  437.0 4.9 %scatter-add.86 = f32[9,6,6,6,128]{4,3,2,0,1:T(8,128)} dynamic-update-slice(f32[9,6,6,6,128]{4,3,2,0,1:T(8,128)} %copy.24329, f32[9,6,6,1,128]{4,3,2,0,1:T(1,128)S(1)} %fusion.173, s32[]{:T(128)} %constant.580.clone.1, s32[]{:T(128)} %constant.580.clone.1, s32[]{:T(128)} %constant.580.clone.1, s32[]{:T(128)} %constant.589.clone.1, s32[]{:T(128)} %constant.580.clone.1) | dynamic-update-slice | bytes 331780 | tf_op jit(solution)/shard_map/scatter-add | solution.py:290
  443.5 4.9 %scatter-add.89 = f32[9,6,6,6,128]{4,3,2,0,1:T(8,128)} dynamic-update-slice(f32[9,6,6,6,128]{4,3,2,0,1:T(8,128)} %scatter-add.86, f32[9,6,6,1,128]{4,3,2,0,1:T(1,128)S(1)} %slice_add_fusion.6, s32[]{:T(128)} %constant.580.clone.1, s32[]{:T(128)} %constant.580.clone.1, s32[]{:T(128)} %constant.580.clone.1, s32[]{:T(128)} %constant.580.clone.1, s32[]{:T(128)} %constant.580.clone.1) | dynamic-update-slice | bytes 331780 | tf_op jit(solution)/shard_map/scatter-add | solution.py:291
  448.4 1.7 fusion.5
  450.1 2.0 copy.24361
  (1199 shorter events, 208.6 us)
Async XLA Ops:
  0.6 8.1 %copy-start = (f32[9,6,6,6,1,128]{5,4,3,2,1,0:T(1,128)S(1)}, f32[9,6,6,6,1,128]{5,4,3,2,1,0:T(1,128)}, u32[]{:S(2)}) copy-start(f32[9,6,6,6,1,128]{5,4,3,2,1,0:T(1,128)} %param.77) | copy-start | bytes 2985988
  3.0 179.7 %collective-permute-start.1 = (f32[9,6,6,128]{3,1,2,0:T(8,128)}, f32[9,6,6,128]{3,1,2,0:T(8,128)}, u32[]{:S(2)}, u32[]{:S(2)}) collective-permute-start(f32[9,6,6,128]{3,1,2,0:T(8,128)} %get-tuple-element.580), channel_id=1, source_target_pairs={{0,8},{8,16},{16,24},{24,32},{32,40},{40,48},{48,56},{56,64},{64,7... | collective-permute-start | bytes 497672 | tf_op jit(solution)/shard_map/ppermute | solution.py:22
  6.8 175.9 %collective-permute-start = (f32[9,6,6,128]{3,1,2,0:T(8,128)}, f32[9,6,6,128]{3,1,2,0:T(8,128)}, u32[]{:S(2)}, u32[]{:S(2)}) collective-permute-start(f32[9,6,6,128]{3,1,2,0:T(8,128)} %get-tuple-element.581), channel_id=1, source_target_pairs={{8,0},{16,8},{24,16},{32,24},{40,32},{48,40},{56,48},{64,56},{72,6... | collective-permute-start | bytes 497672 | tf_op jit(solution)/shard_map/ppermute | solution.py:22
  11.2 165.0 %collective-permute-start.3 = (f32[9,6,6,1,32]{4,3,2,1,0:T(1,128)}, f32[9,6,6,1,32]{4,3,2,1,0:T(1,128)}, u32[]{:S(2)}, u32[]{:S(2)}) collective-permute-start(f32[9,6,6,1,32]{4,3,2,1,0:T(1,128)} %slice_bitcast_fusion.46), channel_id=1, source_target_pairs={{0,1},{1,2},{2,3},{3,4},{4,5},{5,6},{6,7},{8,9},{9,10},{10,11},{11... | collective-permute-start | bytes 124424 | tf_op jit(solution)/shard_map/ppermute | solution.py:22
  21.3 152.4 %collective-permute-start.2 = (f32[9,6,6,1,32]{4,3,2,1,0:T(1,128)}, f32[9,6,6,1,32]{4,3,2,1,0:T(1,128)}, u32[]{:S(2)}, u32[]{:S(2)}) collective-permute-start(f32[9,6,6,1,32]{4,3,2,1,0:T(1,128)} %slice_bitcast_fusion.47), channel_id=1, source_target_pairs={{1,0},{2,1},{3,2},{4,3},{5,4},{6,5},{7,6},{9,8},{10,9},{11,10},{12... | collective-permute-start | bytes 124424 | tf_op jit(solution)/shard_map/ppermute | solution.py:22
  26.0 38.7 %copy-start.236 = (pred[128]{0:T(512)(128)(4,1)}, pred[128]{0:T(512)(128)(4,1)S(1)}, u32[]{:S(2)}) copy-start(pred[128]{0:T(512)(128)(4,1)S(1)} %get-tuple-element.710) | copy-start | bytes 388
  48.3 9.7 %copy-start.281 = (pred[128]{0:T(512)(128)(4,1)S(1)}, pred[128]{0:T(512)(128)(4,1)}, u32[]{:S(2)}) copy-start(pred[128]{0:T(512)(128)(4,1)} %get-tuple-element.708) | copy-start | bytes 388
  64.7 8.6 %copy-start.216 = (f32[1,6,1,6,128]{4,2,1,3,0:T(1,128)S(1)}, f32[1,6,1,6,128]{4,2,1,3,0:T(1,128)}, u32[]{:S(2)}) copy-start(f32[1,6,1,6,128]{4,2,1,3,0:T(1,128)} %get-tuple-element.563) | copy-start | bytes 55300
  64.7 8.6 %copy-start.217 = (f32[1,6,1,6,128]{4,2,1,3,0:T(1,128)S(1)}, f32[1,6,1,6,128]{4,2,1,3,0:T(1,128)}, u32[]{:S(2)}) copy-start(f32[1,6,1,6,128]{4,2,1,3,0:T(1,128)} %get-tuple-element.564) | copy-start | bytes 55300
  64.7 11.2 %copy-start.298 = (f32[6,6,1,1,1]{1,0,4,2,3:T(8,128)S(1)}, f32[6,6,1,1,1]{1,0,4,2,3:T(8,128)}, u32[]{:S(2)}) copy-start(f32[6,6,1,1,1]{1,0,4,2,3:T(8,128)} %constant.614) | copy-start | bytes 436
  81.1 86.9 %copy-start.111 = (f32[1,6,6,128]{3,1,2,0:T(8,128)}, f32[1,6,6,128]{3,1,2,0:T(8,128)S(1)}, u32[]{:S(2)}) copy-start(f32[1,6,6,128]{3,1,2,0:T(8,128)S(1)} %add_maximum_fusion.15) | copy-start | bytes 55300
  214.0 19.9 %copy-start.31 = (f32[9,1,6,6,128]{4,3,2,0,1:T(8,128)}, f32[9,1,6,6,128]{4,3,2,0,1:T(8,128)S(1)}, u32[]{:S(2)}) copy-start(f32[9,1,6,6,128]{4,3,2,0,1:T(8,128)S(1)} %get-tuple-element.539) | copy-start | bytes 497668
  214.0 24.1 %copy-start.33 = (f32[9,6,6,128]{3,2,1,0:T(8,128)}, f32[9,6,6,128]{3,2,1,0:T(8,128)S(1)}, u32[]{:S(2)}) copy-start(f32[9,6,6,128]{3,2,1,0:T(8,128)S(1)} %get-tuple-element.540) | copy-start | bytes 497668
  234.6 66.7 %collective-permute-start.5 = (f32[9,6,6,128]{3,1,2,0:T(8,128)}, f32[9,6,6,128]{3,1,2,0:T(8,128)}, u32[]{:S(2)}, u32[]{:S(2)}) collective-permute-start(f32[9,6,6,128]{3,1,2,0:T(8,128)} %bitcast.3207), channel_id=1, source_target_pairs={{0,8},{8,16},{16,24},{24,32},{32,40},{40,48},{48,56},{56,64},{64,7... | collective-permute-start | bytes 497672 | tf_op jit(solution)/shard_map/ppermute | solution.py:22
  238.8 64.2 %collective-permute-start.4 = (f32[9,6,6,128]{3,1,2,0:T(8,128)}, f32[9,6,6,128]{3,1,2,0:T(8,128)}, u32[]{:S(2)}, u32[]{:S(2)}) collective-permute-start(f32[9,6,6,128]{3,1,2,0:T(8,128)} %copy.23830), channel_id=1, source_target_pairs={{8,0},{16,8},{24,16},{32,24},{40,32},{48,40},{56,48},{64,56},{72,6... | collective-permute-start | bytes 497672 | tf_op jit(solution)/shard_map/ppermute | solution.py:22
  244.8 15.6 %copy-start.50 = (f32[9,6,1,6,128]{4,2,3,0,1:T(1,128)S(1)}, f32[9,6,1,6,128]{4,2,3,0,1:T(1,128)}, u32[]{:S(2)}) copy-start(f32[9,6,1,6,128]{4,2,3,0,1:T(1,128)} %get-tuple-element.518) | copy-start | bytes 497668
  244.8 45.4 %collective-permute-start.7 = (f32[9,6,6,1,32]{4,3,2,1,0:T(1,128)}, f32[9,6,6,1,32]{4,3,2,1,0:T(1,128)}, u32[]{:S(2)}, u32[]{:S(2)}) collective-permute-start(f32[9,6,6,1,32]{4,3,2,1,0:T(1,128)} %slice_bitcast_fusion.44), channel_id=1, source_target_pairs={{0,1},{1,2},{2,3},{3,4},{4,5},{5,6},{6,7},{8,9},{9,10},{10,11},{11... | collective-permute-start | bytes 124424 | tf_op jit(solution)/shard_map/ppermute | solution.py:22
  251.0 10.3 %copy-start.268 = (f32[9]{0:T(128)S(1)}, f32[9]{0:T(128)}, u32[]{:S(2)}) copy-start(f32[9]{0:T(128)} %constant.606.clone) | copy-start | bytes 112
  251.0 10.3 %copy-start.270 = (pred[128]{0:T(512)(128)(4,1)S(1)}, pred[128]{0:T(512)(128)(4,1)}, u32[]{:S(2)}) copy-start(pred[128]{0:T(512)(128)(4,1)} %eq.321) | copy-start | bytes 388
  252.1 9.1 %copy-start.273 = (pred[128]{0:T(512)(128)(4,1)S(1)}, pred[128]{0:T(512)(128)(4,1)}, u32[]{:S(2)}) copy-start(pred[128]{0:T(512)(128)(4,1)} %eq.318) | copy-start | bytes 388
  252.1 9.1 %copy-start.277 = (f32[9]{0:T(128)S(1)}, f32[9]{0:T(128)}, u32[]{:S(2)}) copy-start(f32[9]{0:T(128)} %constant.608.clone) | copy-start | bytes 112
  252.2 9.2 %copy-start.288 = (pred[128]{0:T(512)(128)(4,1)S(1)}, pred[128]{0:T(512)(128)(4,1)}, u32[]{:S(2)}) copy-start(pred[128]{0:T(512)(128)(4,1)} %copy-done.286) | copy-start | bytes 388
  252.2 9.2 %copy-start.294 = (pred[128]{0:T(512)(128)(4,1)S(1)}, pred[128]{0:T(512)(128)(4,1)}, u32[]{:S(2)}) copy-start(pred[128]{0:T(512)(128)(4,1)} %copy-done.292) | copy-start | bytes 388
  254.0 8.0 %copy-start.209 = (f32[1,6,6,1,128]{4,3,2,0,1:T(1,128)S(1)}, f32[1,6,6,1,128]{4,3,2,0,1:T(1,128)}, u32[]{:S(2)}) copy-start(f32[1,6,6,1,128]{4,3,2,0,1:T(1,128)} %get-tuple-element.483) | copy-start | bytes 55300
  254.1 8.0 %copy-start.210 = (f32[1,6,6,1,128]{4,3,2,0,1:T(1,128)S(1)}, f32[1,6,6,1,128]{4,3,2,0,1:T(1,128)}, u32[]{:S(2)}) copy-start(f32[1,6,6,1,128]{4,3,2,0,1:T(1,128)} %get-tuple-element.484) | copy-start | bytes 55300
  254.1 8.0 %copy-start.211 = (f32[1,6,6,1,128]{4,3,2,0,1:T(1,128)S(1)}, f32[1,6,6,1,128]{4,3,2,0,1:T(1,128)}, u32[]{:S(2)}) copy-start(f32[1,6,6,1,128]{4,3,2,0,1:T(1,128)} %get-tuple-element.485) | copy-start | bytes 55300
  254.1 8.0 %copy-start.212 = (f32[1,6,6,1,128]{4,3,2,0,1:T(1,128)S(1)}, f32[1,6,6,1,128]{4,3,2,0,1:T(1,128)}, u32[]{:S(2)}) copy-start(f32[1,6,6,1,128]{4,3,2,0,1:T(1,128)} %get-tuple-element.486) | copy-start | bytes 55300
  254.1 8.0 %copy-start.213 = (f32[1,6,6,1,128]{4,3,2,0,1:T(1,128)S(1)}, f32[1,6,6,1,128]{4,3,2,0,1:T(1,128)}, u32[]{:S(2)}) copy-start(f32[1,6,6,1,128]{4,3,2,0,1:T(1,128)} %get-tuple-element.487) | copy-start | bytes 55300
  254.1 8.0 %copy-start.214 = (f32[1,6,6,1,128]{4,3,2,0,1:T(1,128)S(1)}, f32[1,6,6,1,128]{4,3,2,0,1:T(1,128)}, u32[]{:S(2)}) copy-start(f32[1,6,6,1,128]{4,3,2,0,1:T(1,128)} %get-tuple-element.488) | copy-start | bytes 55300
  254.1 39.2 %collective-permute-start.6 = (f32[9,6,6,1,32]{4,3,2,1,0:T(1,128)}, f32[9,6,6,1,32]{4,3,2,1,0:T(1,128)}, u32[]{:S(2)}, u32[]{:S(2)}) collective-permute-start(f32[9,6,6,1,32]{4,3,2,1,0:T(1,128)} %slice_bitcast_fusion.45), channel_id=1, source_target_pairs={{1,0},{2,1},{3,2},{4,3},{5,4},{6,5},{7,6},{9,8},{10,9},{11,10},{12... | collective-permute-start | bytes 124424 | tf_op jit(solution)/shard_map/ppermute | solution.py:22
  262.2 10.5 %copy-start.113 = (f32[1,6,6,128]{3,2,1,0:T(8,128)}, f32[1,6,6,128]{3,2,1,0:T(8,128)S(1)}, u32[]{:S(2)}) copy-start(f32[1,6,6,128]{3,2,1,0:T(8,128)S(1)} %add_maximum_fusion.7) | copy-start | bytes 55300
  307.9 8.7 %copy-start.43 = (f32[9,6,6,1,128]{4,2,3,0,1:T(8,128)S(1)}, f32[9,6,6,1,128]{4,2,3,0,1:T(8,128)}, u32[]{:S(2)}) copy-start(f32[9,6,6,1,128]{4,2,3,0,1:T(8,128)} %copy-done.42) | copy-start | bytes 497668
  307.9 8.7 %copy-start.90 = (f32[9,6,6,1,127]{4,2,1,0,3:T(8,128)S(1)}, f32[9,6,6,1,127]{4,2,1,0,3:T(8,128)}, u32[]{:S(2)}) copy-start(f32[9,6,6,1,127]{4,2,1,0,3:T(8,128)} %slice_bitcast_fusion.17) | copy-start | bytes 493780
  307.9 8.7 %copy-start.156 = (f32[6,6,128]{2,1,0:T(8,128)S(1)}, f32[6,6,128]{2,1,0:T(8,128)}, u32[]{:S(2)}) copy-start(f32[6,6,128]{2,1,0:T(8,128)} %get-tuple-element.311) | copy-start | bytes 55300
  307.9 8.7 %copy-start.278 = (f32[9]{0:T(128)S(1)}, f32[9]{0:T(128)}, u32[]{:S(2)}) copy-start(f32[9]{0:T(128)} %constant.608.clone) | copy-start | bytes 112
  307.9 8.7 %copy-start.284 = (pred[128]{0:T(512)(128)(4,1)S(1)}, pred[128]{0:T(512)(128)(4,1)}, u32[]{:S(2)}) copy-start(pred[128]{0:T(512)(128)(4,1)} %get-tuple-element.708) | copy-start | bytes 388
  308.0 8.7 %copy-start.289 = (pred[128]{0:T(512)(128)(4,1)S(1)}, pred[128]{0:T(512)(128)(4,1)}, u32[]{:S(2)}) copy-start(pred[128]{0:T(512)(128)(4,1)} %copy-done.286) | copy-start | bytes 388
  308.0 8.7 %copy-start.295 = (pred[128]{0:T(512)(128)(4,1)S(1)}, pred[128]{0:T(512)(128)(4,1)}, u32[]{:S(2)}) copy-start(pred[128]{0:T(512)(128)(4,1)} %copy-done.292) | copy-start | bytes 388
  329.5 16.5 %copy-start.1 = (f32[9,6,6,6,1,128]{5,3,2,0,1,4:T(8,128)}, f32[9,6,6,6,1,128]{5,3,2,0,1,4:T(8,128)S(1)}, u32[]{:S(2)}) copy-start(f32[9,6,6,6,1,128]{5,3,2,0,1,4:T(8,128)S(1)} %fusion.6) | copy-start | bytes 2985988
  351.1 64.0 %collective-permute-start.9 = (f32[9,6,6,128]{3,2,1,0:T(8,128)}, f32[9,6,6,128]{3,2,1,0:T(8,128)}, u32[]{:S(2)}, u32[]{:S(2)}) collective-permute-start(f32[9,6,6,128]{3,2,1,0:T(8,128)} %get-tuple-element.462), channel_id=1, source_target_pairs={{0,8},{8,16},{16,24},{24,32},{32,40},{40,48},{48,56},{56,64},{64,7... | collective-permute-start | bytes 497672 | tf_op jit(solution)/shard_map/ppermute | solution.py:22
  357.4 57.7 %collective-permute-start.8 = (f32[9,6,6,128]{3,2,1,0:T(8,128)}, f32[9,6,6,128]{3,2,1,0:T(8,128)}, u32[]{:S(2)}, u32[]{:S(2)}) collective-permute-start(f32[9,6,6,128]{3,2,1,0:T(8,128)} %get-tuple-element.463), channel_id=1, source_target_pairs={{8,0},{16,8},{24,16},{32,24},{40,32},{48,40},{56,48},{64,56},{72,6... | collective-permute-start | bytes 497672 | tf_op jit(solution)/shard_map/ppermute | solution.py:22
  363.4 20.6 %copy-start.215 = (f32[1,6,6,1,128]{4,3,2,0,1:T(1,128)S(1)}, f32[1,6,6,1,128]{4,3,2,0,1:T(1,128)}, u32[]{:S(2)}) copy-start(f32[1,6,6,1,128]{4,3,2,0,1:T(1,128)} %get-tuple-element.408) | copy-start | bytes 55300
  363.4 42.2 %collective-permute-start.11 = (f32[9,6,6,1,32]{4,3,2,1,0:T(1,128)}, f32[9,6,6,1,32]{4,3,2,1,0:T(1,128)}, u32[]{:S(2)}, u32[]{:S(2)}) collective-permute-start(f32[9,6,6,1,32]{4,3,2,1,0:T(1,128)} %slice_bitcast_fusion.42), channel_id=1, source_target_pairs={{0,1},{1,2},{2,3},{3,4},{4,5},{5,6},{6,7},{8,9},{9,10},{10,11},{11... | collective-permute-start | bytes 124424 | tf_op jit(solution)/shard_map/ppermute | solution.py:22
  369.4 15.6 %copy-start.269 = (f32[9]{0:T(128)S(1)}, f32[9]{0:T(128)}, u32[]{:S(2)}) copy-start(f32[9]{0:T(128)} %constant.606.clone) | copy-start | bytes 112
  369.4 15.6 %copy-start.271 = (pred[128]{0:T(512)(128)(4,1)S(1)}, pred[128]{0:T(512)(128)(4,1)}, u32[]{:S(2)}) copy-start(pred[128]{0:T(512)(128)(4,1)} %eq.321) | copy-start | bytes 388
  369.4 15.6 %copy-start.274 = (pred[128]{0:T(512)(128)(4,1)S(1)}, pred[128]{0:T(512)(128)(4,1)}, u32[]{:S(2)}) copy-start(pred[128]{0:T(512)(128)(4,1)} %eq.318) | copy-start | bytes 388
  371.5 14.6 %copy-start.239 = (pred[128]{0:T(512)(128)(4,1)S(1)}, pred[128]{0:T(512)(128)(4,1)}, u32[]{:S(2)}) copy-start(pred[128]{0:T(512)(128)(4,1)} %copy-done.236) | copy-start | bytes 388
  373.3 34.1 %collective-permute-start.10 = (f32[9,6,6,1,32]{4,3,2,1,0:T(1,128)}, f32[9,6,6,1,32]{4,3,2,1,0:T(1,128)}, u32[]{:S(2)}, u32[]{:S(2)}) collective-permute-start(f32[9,6,6,1,32]{4,3,2,1,0:T(1,128)} %slice_bitcast_fusion.43), channel_id=1, source_target_pairs={{1,0},{2,1},{3,2},{4,3},{5,4},{6,5},{7,6},{9,8},{10,9},{11,10},{12... | collective-permute-start | bytes 124424 | tf_op jit(solution)/shard_map/ppermute | solution.py:22
  (296 other events, 804.8 us)
where the time goes:
time: 462 us; the launch traced here: 453 us
  local copies, waits for them, and re-layouts  205 us (44%)
  other arithmetic  83.5 us (18%)
  blocking collectives  78.5 us (17%)
  starting transfers between devices  50.6 us (11%)
  matrix products  25.8 us (6%)
  between operations  10.3 us (2%)
    pmax x1, blocking collectives, on_device(): fastest = lax.pmax(local_fastest, ('len', 'wid'))  78.5 us
    ppermute x12, starting transfers between devices, shifted(): return lax.ppermute(array, axis, pairs)  50.6 us
    scatter-add x8, local copies, waits for them, and re-layouts, operator(): accumulated.at[low_index].add((low_flux - interface_low) / END_WEIGHT)  29.2 us
    unnamed x741, local copies, waits for them, and re-layouts  25.7 us
    concatenate x23, local copies, waits for them, and re-layouts, operator(): jnp.roll(inner, -stride[direction], axis=-1)  20.8 us
    scatter-add x7, local copies, waits for them, and re-layouts, operator(): accumulated.at[high_index].add((interface_high - high_flux) / END_WEIGHT)  20.3 us
    concatenate x26, local copies, waits for them, and re-layouts, operator(): jnp.roll(inner, stride[direction], axis=-1)  18.5 us
    unnamed x150, other arithmetic  13.8 us
  transfers between devices with their start and end apart: 12, of which 0 were waited for; matrix products, arithmetic and copies ran while one was open for 37% of the time, Pallas kernels for 0%

commit v1 on v0

v1 whole, which is shorter than its diff:
```python
import functools

import jax
import jax.numpy as jnp
import numpy as np
from jax import lax
from jax.experimental import pallas as pl
from jax.experimental.pallas import tpu as pltpu
from jax.sharding import PartitionSpec as P

MESH = pl.DeviceIdType.MESH

EZ = 32
LANES = 128
NODES = 216
PADDED = 224
FACE = 36
HALO = 40
PACK = 9

GAMMA = 5.0 / 3.0
GLM_SPEED = 2.0
JET_SPEED = 0.8
BRAKE_FIELD = 1.0
CFL_NUMBER = 0.1
LIFT = 30.0

STAGES = ((0.0, 1.0, 1.0), (0.75, 0.25, 0.25), (1.0 / 3.0, 2.0 / 3.0, 2.0 / 3.0))


def lgl_derivative():
    points = np.array(
        [
            -1.0,
            -0.7650553239294647,
            -0.2852315164806451,
            0.2852315164806451,
            0.7650553239294647,
            1.0,
        ]
    )
    count = points.shape[0]
    barycentric = np.ones(count)
    for row in range(count):
        for column in range(count):
            if row != column:
                barycentric[row] = barycentric[row] / (points[row] - points[column])
    matrix = np.zeros((count, count))
    for row in range(count):
        for column in range(count):
            if row != column:
                matrix[row, column] = (
                    barycentric[column] / barycentric[row] / (points[row] - points[column])
                )
    for row in range(count):
        matrix[row, row] = -np.sum(matrix[row])
    return matrix.astype(np.float32)


def volume_matrix():
    line = lgl_derivative().astype(np.float64)
    line[0, 0] += LIFT / 2
    line[5, 5] -= LIFT / 2
    line = -2.0 * line
    eye = np.eye(6)
    whole = np.zeros((PADDED, 3 * PADDED))
    whole[:NODES, :NODES] = np.kron(np.kron(line, eye), eye)
    whole[:NODES, PADDED : PADDED + NODES] = np.kron(np.kron(eye, line), eye)
    whole[:NODES, 2 * PADDED : 2 * PADDED + NODES] = np.kron(np.kron(eye, eye), line)
    whole = whole.astype(np.float32)
    high = whole.astype(jnp.bfloat16)
    low = (whole - high.astype(np.float32)).astype(jnp.bfloat16)
    return np.stack([high, low])


def root(x):
    return x * lax.rsqrt(jnp.maximum(x, 1e-30))


def primitives(u):
    inverse = 1.0 / u[0]
    velocity = [u[1] * inverse, u[2] * inverse, u[3] * inverse]
    kinetic = u[1] * velocity[0] + u[2] * velocity[1] + u[3] * velocity[2]
    squares = [u[5] * u[5], u[6] * u[6], u[7] * u[7]]
    field_sq = squares[0] + squares[1] + squares[2]
    pressure = (GAMMA - 1.0) * (u[4] - 0.5 * (kinetic + field_sq + u[8] * u[8]))
    return inverse, velocity, squares, field_sq, pressure


def fast_terms(prims):
    _, _, _, field_sq, pressure = prims
    acoustic = GAMMA * pressure
    gap = acoustic - field_sq
    return acoustic + field_sq, gap * gap, 4.0 * acoustic


def speed_along(prims, terms, d):
    inverse, velocity, squares, _, _ = prims
    both, gap_sq, acoustic4 = terms
    across = squares[(d + 1) % 3] + squares[(d + 2) % 3]
    inner = both + root(gap_sq + acoustic4 * across)
    return jnp.maximum(jnp.abs(velocity[d]) + root(0.5 * inverse * inner), GLM_SPEED)


def face_side(u, d):
    prims = primitives(u)
    _, velocity, _, field_sq, pressure = prims
    field = u[5:8]
    total = pressure + 0.5 * field_sq
    v, b = velocity[d], field[d]
    dot = velocity[0] * field[0] + velocity[1] * field[1] + velocity[2] * field[2]
    twice = GLM_SPEED * u[8]
    flux = [u[1 + d]]
    for c in range(3):
        entry = u[1 + c] * v - field[c] * b
        flux.append(entry + total if c == d else entry)
    flux.append(v * (u[4] + total) + b * (twice - dot))
    for c in range(3):
        flux.append(twice if c == d else v * field[c] - b * velocity[c])
    flux.append(GLM_SPEED * b)
    return flux, speed_along(prims, fast_terms(prims), d)


def face_flux(left, right, d):
    left_flux, left_speed = face_side(left, d)
    right_flux, right_speed = face_side(right, d)
    half = LIFT / 2
    largest = half * jnp.maximum(left_speed, right_speed)
    return [
        half * (left_flux[c] + right_flux[c]) - largest * (right[c] - left[c]) for c in range(9)
    ]


def inflow_value(c, d, outward):
    if c == 0:
        return 1.0
    if c == 1 + d:
        return -outward * JET_SPEED
    if c == 4:
        return 1.0 / (GAMMA - 1.0) + 0.5 * JET_SPEED**2 + 0.5 * BRAKE_FIELD**2
    if c == 7:
        return BRAKE_FIELD
    return 0.0


def with_outer(inner, interior, code, d, outward):
    states = []
    for c in range(9):
        x = interior[c]
        if c == 1 + d:
            x = jnp.where(code == 1, -x, x)
        x = jnp.where(code == 0, inflow_value(c, d, outward), x)
        states.append(x if inner is None else jnp.where(code < 3, x, inner[c]))
    return states


CHUNKS = ((0, 16), (16, 16), (32, 4))


def kernel(
    nlen,
    nwid,
    u_hbm,
    mat_hbm,
    ends_ref,
    sides_ref,
    walls_ref,
    out_ref,
    dt_ref,
    u0,
    u1,
    u2,
    mat,
    fhi,
    flo,
    acc,
    above,
    below,
    own_low,
    own_high,
    wide_below,
    wide_above,
    t_low,
    t_high,
    g_wide,
    e_low,
    e_high,
    peak,
    peak_group,
    peak_all,
    load_sem,
    send_sem,
    recv_sem,
    peak_send,
    peak_recv,
):
    li = lax.axis_index("len")
    wi = lax.axis_index("wid")
    group = max(nlen // 2, 1)
    blocks = nlen // group
    crowd = blocks * nwid
    lanes = lax.broadcasted_iota(jnp.int32, (1, LANES), 1)
    states = (u0, u1, u2)

    load_u = pltpu.make_async_copy(u_hbm, u0.at[:, pl.ds(0, NODES), :], load_sem.at[0])
    load_m = pltpu.make_async_copy(mat_hbm, mat, load_sem.at[1])
    load_u.start()
    load_m.start()

    in_group = lax.rem(li, group)
    block = li // group
    base = block * group
    in_crowd = block * nwid + wi

    def group_peer(step):
        return (base + lax.rem(in_group + step, group), wi)

    def crowd_peer(step):
        other = lax.rem(in_crowd + step, crowd)
        return ((other // nwid) * group + in_group, lax.rem(other, nwid))

    barrier = pltpu.get_barrier_semaphore()

    def greet(peer):
        pl.semaphore_signal(barrier, inc=1, device_id=peer, device_id_type=MESH)

    has_prev, has_next = li > 0, li < nlen - 1
    has_left, has_right = wi > 0, wi < nwid - 1

    @pl.when(has_prev)
    def _():
        greet((li - 1, wi))

    @pl.when(has_next)
    def _():
        greet((li + 1, wi))

    @pl.loop(1, group)
    def _(step):
        greet(group_peer(step))

    @pl.loop(1, crowd)
    def _(step):
        greet(crowd_peer(step))

    for ref in states:
        for c in range(9):
            ref[c, pl.ds(NODES, 8), :] = jnp.ones((8, LANES), jnp.float32)

    z = lanes % EZ
    y = lanes // EZ
    wide = LANES // EZ

    def tiled(row):
        return jnp.concatenate([row] * wide, axis=1)

    def wall_row(side):
        row = walls_ref[side]
        parts = [jnp.broadcast_to(row[:, q : q + 1], (1, EZ)) for q in range(wide)]
        return jnp.concatenate(parts, axis=1)

    def ends_row(side):
        return jnp.concatenate([ends_ref[side, q : q + 1, :] for q in range(wide)], axis=1)

    low_wall = jnp.where(z == 0, wall_row(0), 3)
    high_wall = wall_row(1)

    load_u.wait()
    neighbours = (
        has_prev.astype(jnp.int32)
        + has_next.astype(jnp.int32)
    )
    pl.semaphore_wait(barrier, group - 1 + crowd - 1 + neighbours)

    def copy_prev(s):
        return pltpu.make_async_remote_copy(
            src_ref=states[s].at[:, pl.ds(0, HALO), :],
            dst_ref=above.at[s],
            send_sem=send_sem.at[s, 0],
            recv_sem=recv_sem.at[s, 0],
            device_id=(li - 1, wi),
            device_id_type=MESH,
        )

    def copy_next(s):
        return pltpu.make_async_remote_copy(
            src_ref=states[s].at[:, pl.ds(NODES - HALO, HALO), :],
            dst_ref=below.at[s],
            send_sem=send_sem.at[s, 1],
            recv_sem=recv_sem.at[s, 1],
            device_id=(li + 1, wi),
            device_id_type=MESH,
        )

    def copy_left(s):
        return pltpu.make_async_remote_copy(
            src_ref=own_low.at[s],
            dst_ref=wide_above.at[s],
            send_sem=send_sem.at[s, 2],
            recv_sem=recv_sem.at[s, 2],
            device_id=(li, wi - 1),
            device_id_type=MESH,
        )

    def copy_right(s):
        return pltpu.make_async_remote_copy(
            src_ref=own_high.at[s],
            dst_ref=wide_below.at[s],
            send_sem=send_sem.at[s, 3],
            recv_sem=recv_sem.at[s, 3],
            device_id=(li, wi + 1),
            device_id_type=MESH,
        )

    def roll(x, by):
        by = by % LANES
        return x if by == 0 else pltpu.roll(x, by, axis=1)

    def packed(ref):
        return [ref[pl.ds(c, PACK, stride=9), :] for c in range(9)]

    def send(s):
        u = states[s]

        @pl.when(has_prev)
        def _():
            copy_prev(s).start()

        @pl.when(has_next)
        def _():
            copy_next(s).start()

        for c in range(9):
            for i in range(6):
                t_low[c, pl.ds(6 * i, 6), :] = u[c, pl.ds(36 * i, 6), :]
                t_high[c, pl.ds(6 * i, 6), :] = u[c, pl.ds(36 * i + 30, 6), :]
        for ref, dest, first in ((t_low, own_low, 0), (t_high, own_high, wide - 1)):
            for c in range(9):
                whole = None
                for q in range(wide):
                    piece = roll(ref[c, pl.ds(q, PACK, stride=4), :], EZ * (q - first))
                    whole = piece if q == 0 else jnp.where(y == q, piece, whole)
                dest[s, pl.ds(c, PACK, stride=9), :] = whole

        @pl.when(has_left)
        def _():
            copy_left(s).start()

        @pl.when(has_right)
        def _():
            copy_right(s).start()

    def volume(s):
        u_ref = states[s]

        def put(d, c, parts):
            fhi[pl.ds(rows[d], 16), pl.ds(c * LANES, LANES)] = parts[0]
            flo[pl.ds(rows[d], 16), pl.ds(c * LANES, LANES)] = parts[1]

        def split(x):
            high = x.astype(jnp.bfloat16)
            return high, (x - high.astype(jnp.float32)).astype(jnp.bfloat16)

        rows = [None] * 3

        def body(chunk, _):
            start = pl.multiple_of(chunk * 16, 16)
            for d in range(3):
                rows[d] = pl.multiple_of(d * PADDED + chunk * 16, 16)
            u = [u_ref[c, pl.ds(start, 16), :] for c in range(9)]
            prims = primitives(u)
            _, velocity, _, field_sq, pressure = prims
            field = u[5:8]
            total = pressure + 0.5 * field_sq
            enthalpy = u[4] + total
            twice = GLM_SPEED * u[8]
            back = twice - (
                velocity[0] * field[0] + velocity[1] * field[1] + velocity[2] * field[2]
            )
            psi_parts = split(twice)
            for d in range(3):
                put(d, 0, split(u[1 + d]))
                put(d, 5 + d, psi_parts)
                put(d, 8, split(GLM_SPEED * field[d]))
                put(d, 4, split(velocity[d] * enthalpy + field[d] * back))
                put(d, 1 + d, split(u[1 + d] * velocity[d] - field[d] * field[d] + total))
                for e in range(d + 1, 3):
                    shear = split(u[1 + d] * velocity[e] - field[d] * field[e])
                    put(d, 1 + e, shear)
                    put(e, 1 + d, shear)
                    turn = split(velocity[d] * field[e] - field[d] * velocity[e])
                    put(d, 5 + e, turn)
                    put(e, 5 + d, (-turn[0], -turn[1]))
            if s == 0:
                terms = fast_terms(prims)
                top = speed_along(prims, terms, 0)
                for d in (1, 2):
                    top = jnp.maximum(top, speed_along(prims, terms, d))
                row = lax.broadcasted_iota(jnp.int32, (16, LANES), 0) + start
                top = jnp.where(row < NODES, top, GLM_SPEED)
                peak[...] = jnp.maximum(peak[...], jnp.max(top, axis=0, keepdims=True))
            return 0

        lax.fori_loop(0, PADDED // 16, body, 0)

    def derivatives():
        for first in range(0, 9, 2):
            count = min(2, 9 - first)
            span = pl.ds(first * LANES, count * LANES)
            high = fhi[:, span]
            result = jnp.dot(mat[0], high, preferred_element_type=jnp.float32)
            result += jnp.dot(mat[1], high, preferred_element_type=jnp.float32)
            result += jnp.dot(mat[0], flo[:, span], preferred_element_type=jnp.float32)
            for c in range(count):
                acc[first + c] = result[:, c * LANES : (c + 1) * LANES]

    def inner_faces(s):
        u_ref = states[s]
        for first, count in CHUNKS:
            low_rows = pl.ds(6 * first, count, stride=6)
            high_rows = pl.ds(6 * first + 5, count, stride=6)
            low = [u_ref[c, low_rows, :] for c in range(9)]
            high = [u_ref[c, high_rows, :] for c in range(9)]
            beside = [roll(x, 1) for x in high]
            left = with_outer(beside, low, low_wall, 2, -1.0)
            flux = face_flux(left, low, 2)
            for c in range(9):
                acc[c, low_rows, :] = acc[c, low_rows, :] + flux[c]
            last = face_flux(high, with_outer(None, high, high_wall, 2, 1.0), 2)
            for c in range(9):
                upper = jnp.where(z == EZ - 1, last[c], roll(flux[c], -1))
                acc[c, high_rows, :] = acc[c, high_rows, :] - upper
        for first, count in CHUNKS:
            rows = pl.ds(first, count)
            low = [t_low[c, rows, :] for c in range(9)]
            left = [roll(t_high[c, rows, :], EZ) for c in range(9)]
            flux = face_flux(left, low, 1)
            for c in range(9):
                g_wide[c, rows, :] = flux[c]
        for c in range(9):
            for i in range(6):
                flux = g_wide[c, pl.ds(6 * i, 6), :]
                rows = pl.ds(36 * i, 6)
                acc[c, rows, :] = acc[c, rows, :] + jnp.where(y > 0, flux, 0.0)
                rows = pl.ds(36 * i + 30, 6)
                acc[c, rows, :] = acc[c, rows, :] - jnp.where(y < wide - 1, roll(flux, -EZ), 0.0)

    def width_edges(s):
        @pl.when(has_left)
        def _():
            copy_right(s).wait_recv()

        @pl.when(has_right)
        def _():
            copy_left(s).wait_recv()

        @pl.when(jnp.logical_not(has_left))
        def _():
            outer = with_outer(None, packed(own_low.at[s]), tiled(sides_ref[0]), 1, -1.0)
            for c in range(9):
                wide_below[s, pl.ds(c, PACK, stride=9), :] = outer[c]

        @pl.when(jnp.logical_not(has_right))
        def _():
            outer = with_outer(None, packed(own_high.at[s]), tiled(sides_ref[1]), 1, 1.0)
            for c in range(9):
                wide_above[s, pl.ds(c, PACK, stride=9), :] = outer[c]

        low = face_flux(packed(wide_below.at[s]), packed(own_low.at[s]), 1)
        high = face_flux(packed(own_high.at[s]), packed(wide_above.at[s]), 1)
        for c in range(9):
            for q in range(wide):
                rows = pl.ds(q, PACK, stride=4)
                e_low[c, rows, :] = jnp.where(y == 0, roll(low[c], -EZ * q), 0.0)
                e_high[c, rows, :] = jnp.where(
                    y == wide - 1, roll(high[c], EZ * (wide - 1 - q)), 0.0
                )
        for c in range(9):
            for i in range(6):
                rows = pl.ds(36 * i, 6)
                acc[c, rows, :] = acc[c, rows, :] + e_low[c, pl.ds(6 * i, 6), :]
                rows = pl.ds(36 * i + 30, 6)
                acc[c, rows, :] = acc[c, rows, :] - e_high[c, pl.ds(6 * i, 6), :]

    def length_edges(s):
        u_ref = states[s]
        top = NODES - FACE
        skip = HALO - FACE

        @pl.when(has_prev)
        def _():
            copy_next(s).wait_recv()

        @pl.when(has_next)
        def _():
            copy_prev(s).wait_recv()

        @pl.when(jnp.logical_not(has_prev))
        def _():
            for first, count in CHUNKS:
                own = [u_ref[c, pl.ds(first, count), :] for c in range(9)]
                outer = with_outer(None, own, ends_row(0), 0, -1.0)
                for c in range(9):
                    below[s, c, pl.ds(skip + first, count), :] = outer[c]

        @pl.when(jnp.logical_not(has_next))
        def _():
            for first, count in CHUNKS:
                own = [u_ref[c, pl.ds(top + first, count), :] for c in range(9)]
                outer = with_outer(None, own, ends_row(1), 0, 1.0)
                for c in range(9):
                    above[s, c, pl.ds(first, count), :] = outer[c]

        for first, count in CHUNKS:
            rows = pl.ds(first, count)
            left = [below[s, c, pl.ds(skip + first, count), :] for c in range(9)]
            flux = face_flux(left, [u_ref[c, rows, :] for c in range(9)], 0)
            for c in range(9):
                acc[c, rows, :] = acc[c, rows, :] + flux[c]
        for first, count in CHUNKS:
            rows = pl.ds(top + first, count)
            right = [above[s, c, pl.ds(first, count), :] for c in range(9)]
            flux = face_flux([u_ref[c, rows, :] for c in range(9)], right, 0)
            for c in range(9):
                acc[c, rows, :] = acc[c, rows, :] - flux[c]

    def update(s, step):
        first, own, factor = STAGES[s]
        weight = step * factor
        for c in range(9):
            rows = pl.ds(0, NODES)
            new = own * states[s][c, rows, :] + weight * acc[c, rows, :]
            if first:
                new = new + first * u0[c, rows, :]
            if s < 2:
                states[s + 1][c, rows, :] = new
            else:
                out_ref[c] = new

    def peak_copy(src, dst, which, step, peer):
        return pltpu.make_async_remote_copy(
            src_ref=src,
            dst_ref=dst.at[step - 1],
            send_sem=peak_send.at[which],
            recv_sem=peak_recv.at[which],
            device_id=peer,
            device_id_type=MESH,
        )

    peak[...] = jnp.full((1, LANES), GLM_SPEED, jnp.float32)
    send(0)
    volume(0)

    @pl.loop(1, group)
    def _(step):
        peak_copy(peak, peak_group, 0, step, group_peer(step)).start()

    load_m.wait()
    derivatives()
    pltpu.make_async_copy(peak_group, peak_group, peak_recv.at[0]).wait()
    pltpu.make_async_copy(peak_group, peak_group, peak_send.at[0]).wait()
    peak[...] = jnp.maximum(peak[...], jnp.max(peak_group[...], axis=0))

    @pl.loop(1, crowd)
    def _(step):
        peak_copy(peak, peak_all, 1, step, crowd_peer(step)).start()

    inner_faces(0)
    width_edges(0)
    length_edges(0)
    pltpu.make_async_copy(peak_all, peak_all, peak_recv.at[1]).wait()
    fastest = jnp.max(jnp.maximum(peak[...], jnp.max(peak_all[...], axis=0)), axis=1, keepdims=True)
    step_row = CFL_NUMBER / (11.0 * jnp.broadcast_to(fastest, (1, LANES)))
    dt_ref[0, 0] = jnp.max(step_row)
    update(0, step_row)

    for s in (1, 2):
        send(s)
        volume(s)
        derivatives()
        inner_faces(s)
        width_edges(s)
        length_edges(s)
        update(s, step_row)

    pltpu.make_async_copy(peak_all, peak_all, peak_send.at[1]).wait()
    for s in range(3):
        for have, copy in (
            (has_prev, copy_prev),
            (has_next, copy_next),
            (has_left, copy_left),
            (has_right, copy_right),
        ):

            @pl.when(have)
            def _(copy=copy):
                copy(s).wait_send()


def solution(mesh):
    nlen, nwid = mesh.shape["len"], mesh.shape["wid"]
    group = max(nlen // 2, 1)
    crowd = nlen // group * nwid
    matrix = volume_matrix()

    def on_device(conserved, ends_kind, sides_kind, walls_kind):
        f32 = jnp.float32
        vmem = pl.BlockSpec(memory_space=pltpu.VMEM)
        hbm = pl.BlockSpec(memory_space=pl.ANY)
        state = pltpu.VMEM((9, PADDED, LANES), f32)
        halo = pltpu.VMEM((3, 9, HALO, LANES), f32)
        pack = pltpu.VMEM((3, 9 * PACK, LANES), f32)
        trace = pltpu.VMEM((9, HALO, LANES), f32)
        flux = pltpu.VMEM((3 * PADDED, 9 * LANES), jnp.bfloat16)
        updated, step = pl.pallas_call(
            functools.partial(kernel, nlen, nwid),
            out_shape=(
                jax.ShapeDtypeStruct((9, NODES, LANES), f32),
                jax.ShapeDtypeStruct((1, 1), f32),
            ),
            in_specs=[hbm, hbm, vmem, vmem, vmem],
            out_specs=(vmem, pl.BlockSpec(memory_space=pltpu.SMEM)),
            scratch_shapes=[
                state,
                state,
                state,
                pltpu.VMEM((2, PADDED, 3 * PADDED), jnp.bfloat16),
                flux,
                flux,
                state,
                halo,
                halo,
                pack,
                pack,
                pack,
                pack,
                trace,
                trace,
                trace,
                trace,
                trace,
                pltpu.VMEM((1, LANES), f32),
                pltpu.VMEM((group - 1, 1, LANES), f32),
                pltpu.VMEM((crowd - 1, 1, LANES), f32),
                pltpu.SemaphoreType.DMA((2,)),
                pltpu.SemaphoreType.DMA((3, 4)),
                pltpu.SemaphoreType.DMA((3, 4)),
                pltpu.SemaphoreType.DMA((2,)),
                pltpu.SemaphoreType.DMA((2,)),
            ],
            compiler_params=pltpu.CompilerParams(
                collective_id=0, has_side_effects=True, vmem_limit_bytes=40 * 1024 * 1024
            ),
        )(
            conserved.reshape(9, NODES, LANES),
            jnp.asarray(matrix),
            ends_kind,
            sides_kind,
            walls_kind,
        )
        return updated.reshape(conserved.shape), step.reshape(())

    return jax.shard_map(
        on_device,
        mesh=mesh,
        in_specs=(
            P(None, None, None, None, "len", "wid"),
            P(None, "wid", None),
            P(None, "len", None),
            P(None, "len", "wid"),
        ),
        out_specs=(P(None, None, None, None, "len", "wid"), P()),
        check_vma=False,
    )
```

time: 462 us -> 48.8 us (0.11); the launches traced: 453 us -> 48.2 us
  local copies, waits for them, and re-layouts: 205 us -> 5.29 us
  other arithmetic: 83.5 us -> 0 us
  blocking collectives: 78.5 us -> 0 us
  starting transfers between devices: 50.6 us -> 0 us
  Pallas kernels: 0 us -> 40.6 us
  matrix products: 25.8 us -> 0 us
  between operations: 10.3 us -> 2.34 us
    pmax x1 -> x0, blocking collectives: 78.5 us -> none  [on_device(): fastest = lax.pmax(local_fastest, ('len', 'wid'))]
    ppermute x12 -> x0, starting transfers between devices: 50.6 us -> none  [shifted(): return lax.ppermute(array, axis, pairs)]
    scatter-add x15 -> x0, local copies, waits for them, and re-layouts: 49.6 us -> none  [the longest x8 29.2 us: operator(): accumulated.at[low_index].add((low_flux - interface_low) / END_WEIGHT)]
    pallas_call x0 -> x1, Pallas kernels: none -> 40.6 us  [on_device(): pl.pallas_call(functools.partial(kernel, nlen, nwid), out_shape=(jax.Shap...]
    concatenate x49 -> x0, local copies, waits for them, and re-layouts: 39.3 us -> none  [the longest x23 20.8 us: operator(): jnp.roll(inner, -stride[direction], axis=-1)]
    slice x55 -> x0, local copies, waits for them, and re-layouts: 33 us -> none  [the longest x19 13.6 us: operator(): jnp.roll(inner, stride[direction], axis=-1)]
    dot_general x9 -> x0, matrix products: 25.8 us -> none  [the longest x3 11.7 us: operator(): jnp.einsum('aj,vijke->viake', derivative, fluxes[1], precision=precise)]
    unnamed x741 -> x11, local copies, waits for them, and re-layouts: 25.7 us -> 5.29 us
  transfers between devices with their start and end apart: 12 -> 0, of which waited for: 0 -> 0; matrix products, arithmetic and copies ran while one was open for 37% -> 0% of each run, Pallas kernels for 0% -> 0%
where the time goes in v1:
time: 48.8 us; the launch traced here: 48.2 us
  Pallas kernels  40.6 us (83%)
  local copies, waits for them, and re-layouts  5.29 us (11%)
  between operations  2.34 us (5%)
    pallas_call x1, Pallas kernels, on_device(): pl.pallas_call(functools.partial(kernel, nlen, nwid), out_shape=(jax.Shap...  40.6 us
    unnamed x11, local copies, waits for them, and re-layouts  5.29 us

profile of v1, /device:TPU:27, one launch (start us, length us, event | category | flops | bytes accessed | tf_op | source)
XLA Modules:
  0.0 48.2 jit_solution(5525405556357007715)
XLA Ops:
  0.6 0.0 copy-start.3
  0.6 0.7 %copy-done.3 = s32[2,1,32]{2,1,0:T(1,128)S(1)} copy-done((s32[2,1,32]{2,1,0:T(1,128)S(1)}, s32[2,1,32]{2,1,0:T(1,128)}, u32[]{:S(2)}) %copy-start.3) | copy-done | bytes 280
  1.3 0.0 copy-start
  1.3 1.2 %copy-done = f32[9,6,6,6,1,128]{5,4,3,2,1,0:T(1,128)S(1)} copy-done((f32[9,6,6,6,1,128]{5,4,3,2,1,0:T(1,128)S(1)}, f32[9,6,6,6,1,128]{5,4,3,2,1,0:T(1,128)}, u32[]{:S(2)}) %copy-start) | copy-done | bytes 995352
  2.5 0.0 copy-start.1
  2.5 1.1 %copy-done.1 = bf16[2,224,672]{2,1,0:T(8,128)(2,1)S(1)} copy-done((bf16[2,224,672]{2,1,0:T(8,128)(2,1)S(1)}, bf16[2,224,672]{2,1,0:T(8,128)(2,1)}, u32[]{:S(2)}) %copy-start.1) | copy-done | bytes 602136
  3.6 0.0 copy-start.2
  3.6 0.7 %copy-done.2 = s32[2,4,32]{2,1,0:T(4,128)S(1)} copy-done((s32[2,4,32]{2,1,0:T(4,128)S(1)}, s32[2,4,32]{2,1,0:T(4,128)}, u32[]{:S(2)}) %copy-start.2) | copy-done | bytes 1048
  4.3 0.0 copy-start.4
  4.3 0.7 %copy-done.4 = s32[2,1,4]{2,1,0:T(1,128)S(1)} copy-done((s32[2,1,4]{2,1,0:T(1,128)S(1)}, s32[2,1,4]{2,1,0:T(1,128)}, u32[]{:S(2)}) %copy-start.4) | copy-done | bytes 56
  5.0 40.6 %shard_map.68 = (f32[9,216,128]{2,1,0:T(8,128)S(1)}, f32[1,1]{1,0:T(1,128)}) custom-call(f32[9,216,128]{2,1,0:T(8,128)S(1)} %bitcast.3, bf16[2,224,672]{2,1,0:T(8,128)(2,1)S(1)} %copy-done.1, s32[2,4,32]{2,1,0:T(4,128)S(1)} %copy-done.2, s32[2,1,32]{2,1,0:T(1,128)S(1)} %copy-done.3, s32[2,1,4]{2,1,0:T(1,128)S(1)} %copy-done.4), custom_call_target="tpu_custom_call" | custom-call | tf_op jit(solution)/shard_map/pallas_call | solution.py:615
  45.6 1.0 %copy.11 = f32[9,6,6,6,1,128]{5,4,3,2,1,0:T(1,128)} copy(f32[9,6,6,6,1,128]{5,4,3,2,1,0:T(1,128)S(1)} %bitcast.4) | data formatting | bytes 1990656
Async XLA Ops:
  0.6 0.7 %copy-start.3 = (s32[2,1,32]{2,1,0:T(1,128)S(1)}, s32[2,1,32]{2,1,0:T(1,128)}, u32[]{:S(2)}) copy-start(s32[2,1,32]{2,1,0:T(1,128)} %sides_ref.1) | copy-start | bytes 772
  1.3 1.2 %copy-start = (f32[9,6,6,6,1,128]{5,4,3,2,1,0:T(1,128)S(1)}, f32[9,6,6,6,1,128]{5,4,3,2,1,0:T(1,128)}, u32[]{:S(2)}) copy-start(f32[9,6,6,6,1,128]{5,4,3,2,1,0:T(1,128)} %param.5) | copy-start | bytes 2985988
  2.5 1.1 %copy-start.1 = (bf16[2,224,672]{2,1,0:T(8,128)(2,1)S(1)}, bf16[2,224,672]{2,1,0:T(8,128)(2,1)}, u32[]{:S(2)}) copy-start(bf16[2,224,672]{2,1,0:T(8,128)(2,1)} %constant.2.clone.mat_hbm) | copy-start | bytes 1806340
  3.6 0.7 %copy-start.2 = (s32[2,4,32]{2,1,0:T(4,128)S(1)}, s32[2,4,32]{2,1,0:T(4,128)}, u32[]{:S(2)}) copy-start(s32[2,4,32]{2,1,0:T(4,128)} %ends_ref.1) | copy-start | bytes 3076
  4.3 0.7 %copy-start.4 = (s32[2,1,4]{2,1,0:T(1,128)S(1)}, s32[2,1,4]{2,1,0:T(1,128)}, u32[]{:S(2)}) copy-start(s32[2,1,4]{2,1,0:T(1,128)} %walls_ref.1) | copy-start | bytes 100

commit v2 on v1

--- a/solution.py
+++ b/solution.py
@@ -162,11 +162,14 @@
     nwid,
     u_hbm,
     mat_hbm,
+    ends_hbm,
+    sides_hbm,
+    walls_hbm,
+    out_ref,
+    dt_ref,
     ends_ref,
     sides_ref,
     walls_ref,
-    out_ref,
-    dt_ref,
     u0,
     u1,
     u2,
@@ -183,8 +186,6 @@
     t_low,
     t_high,
     g_wide,
-    e_low,
-    e_high,
     peak,
     peak_group,
     peak_all,
@@ -200,11 +201,19 @@
     blocks = nlen // group
     crowd = blocks * nwid
     lanes = lax.broadcasted_iota(jnp.int32, (1, LANES), 1)
-    states = (u0, u1, u2)
+    states = (u0, u1, u2, out_ref)
 
     load_u = pltpu.make_async_copy(u_hbm, u0.at[:, pl.ds(0, NODES), :], load_sem.at[0])
     load_m = pltpu.make_async_copy(mat_hbm, mat, load_sem.at[1])
     load_u.start()
+    load_kinds = [
+        pltpu.make_async_copy(src, dst, load_sem.at[2 + n])
+        for n, (src, dst) in enumerate(
+            ((ends_hbm, ends_ref), (sides_hbm, sides_ref), (walls_hbm, walls_ref))
+        )
+    ]
+    for load in load_kinds:
+        load.start()
     load_m.start()
 
     in_group = lax.rem(li, group)
@@ -227,6 +236,11 @@
     has_prev, has_next = li > 0, li < nlen - 1
     has_left, has_right = wi > 0, wi < nwid - 1
 
+    for step in range(1, crowd // 2 + 1):
+        greet(crowd_peer(step))
+        if step < crowd - step:
+            greet(crowd_peer(crowd - step))
+
     @pl.when(has_prev)
     def _():
         greet((li - 1, wi))
@@ -239,11 +253,7 @@
     def _(step):
         greet(group_peer(step))
 
-    @pl.loop(1, crowd)
-    def _(step):
-        greet(crowd_peer(step))
-
-    for ref in states:
+    for ref in states[:3]:
         for c in range(9):
             ref[c, pl.ds(NODES, 8), :] = jnp.ones((8, LANES), jnp.float32)
 
@@ -262,15 +272,6 @@
     def ends_row(side):
         return jnp.concatenate([ends_ref[side, q : q + 1, :] for q in range(wide)], axis=1)
 
-    low_wall = jnp.where(z == 0, wall_row(0), 3)
-    high_wall = wall_row(1)
-
-    load_u.wait()
-    neighbours = (
-        has_prev.astype(jnp.int32)
-        + has_next.astype(jnp.int32)
-    )
-    pl.semaphore_wait(barrier, group - 1 + crowd - 1 + neighbours)
 
     def copy_prev(s):
         return pltpu.make_async_remote_copy(
@@ -319,17 +320,26 @@
     def packed(ref):
         return [ref[pl.ds(c, PACK, stride=9), :] for c in range(9)]
 
-    def send(s):
+    def send_width(s):
+        @pl.when(has_left)
+        def _():
+            copy_left(s).start()
+
+        @pl.when(has_right)
+        def _():
+            copy_right(s).start()
+
+    def send_length(s):
+        @pl.when(has_prev)
+        def _():
+            copy_prev(s).start()
+
+        @pl.when(has_next)
+        def _():
+            copy_next(s).start()
+
+    def gather(s):
         u = states[s]
-
-        @pl.when(has_prev)
-        def _():
-            copy_prev(s).start()
-
-        @pl.when(has_next)
-        def _():
-            copy_next(s).start()
-
         for c in range(9):
             for i in range(6):
                 t_low[c, pl.ds(6 * i, 6), :] = u[c, pl.ds(36 * i, 6), :]
@@ -342,13 +352,20 @@
                     whole = piece if q == 0 else jnp.where(y == q, piece, whole)
                 dest[s, pl.ds(c, PACK, stride=9), :] = whole
 
-        @pl.when(has_left)
-        def _():
-            copy_left(s).start()
-
-        @pl.when(has_right)
-        def _():
-            copy_right(s).start()
+    def scatter(s):
+        u = states[s]
+        for ref, src, first in ((t_low, own_low, 0), (t_high, own_high, wide - 1)):
+            for c in range(9):
+                new = src[s, pl.ds(c, PACK, stride=9), :]
+                for q in range(wide):
+                    rows = pl.ds(q, PACK, stride=4)
+                    ref[c, rows, :] = jnp.where(
+                        y == first, roll(new, EZ * (first - q)), ref[c, rows, :]
+                    )
+        for c in range(9):
+            for i in range(6):
+                u[c, pl.ds(36 * i, 6), :] = t_low[c, pl.ds(6 * i, 6), :]
+                u[c, pl.ds(36 * i + 30, 6), :] = t_high[c, pl.ds(6 * i, 6), :]
 
     def volume(s):
         u_ref = states[s]
@@ -391,17 +408,22 @@
                     turn = split(velocity[d] * field[e] - field[d] * velocity[e])
                     put(d, 5 + e, turn)
                     put(e, 5 + d, (-turn[0], -turn[1]))
-            if s == 0:
-                terms = fast_terms(prims)
-                top = speed_along(prims, terms, 0)
-                for d in (1, 2):
-                    top = jnp.maximum(top, speed_along(prims, terms, d))
-                row = lax.broadcasted_iota(jnp.int32, (16, LANES), 0) + start
-                top = jnp.where(row < NODES, top, GLM_SPEED)
-                peak[...] = jnp.maximum(peak[...], jnp.max(top, axis=0, keepdims=True))
             return 0
 
         lax.fori_loop(0, PADDED // 16, body, 0)
+
+    def largest_speed():
+        def body(chunk, top):
+            start = pl.multiple_of(chunk * 8, 8)
+            prims = primitives([u0[c, pl.ds(start, 8), :] for c in range(9)])
+            terms = fast_terms(prims)
+            for d in range(3):
+                top = jnp.maximum(top, speed_along(prims, terms, d))
+            return top
+
+        start = jnp.full((8, LANES), GLM_SPEED, jnp.float32)
+        top = lax.fori_loop(0, NODES // 8, body, start, unroll=3)
+        peak[...] = jnp.max(top, axis=0, keepdims=True)
 
     def derivatives():
         for first in range(0, 9, 2):
@@ -414,7 +436,7 @@
             for c in range(count):
                 acc[first + c] = result[:, c * LANES : (c + 1) * LANES]
 
-    def inner_faces(s):
+    def inner_faces(s, low_wall, high_wall):
         u_ref = states[s]
         for first, count in CHUNKS:
             low_rows = pl.ds(6 * first, count, stride=6)
@@ -445,7 +467,7 @@
                 rows = pl.ds(36 * i + 30, 6)
                 acc[c, rows, :] = acc[c, rows, :] - jnp.where(y < wide - 1, roll(flux, -EZ), 0.0)
 
-    def width_edges(s):
+    def width_edges(s, step_row):
         @pl.when(has_left)
         def _():
             copy_right(s).wait_recv()
@@ -466,21 +488,17 @@
             for c in range(9):
                 wide_above[s, pl.ds(c, PACK, stride=9), :] = outer[c]
 
-        low = face_flux(packed(wide_below.at[s]), packed(own_low.at[s]), 1)
-        high = face_flux(packed(own_high.at[s]), packed(wide_above.at[s]), 1)
-        for c in range(9):
-            for q in range(wide):
-                rows = pl.ds(q, PACK, stride=4)
-                e_low[c, rows, :] = jnp.where(y == 0, roll(low[c], -EZ * q), 0.0)
-                e_high[c, rows, :] = jnp.where(
-                    y == wide - 1, roll(high[c], EZ * (wide - 1 - q)), 0.0
-                )
-        for c in range(9):
-            for i in range(6):
-                rows = pl.ds(36 * i, 6)
-                acc[c, rows, :] = acc[c, rows, :] + e_low[c, pl.ds(6 * i, 6), :]
-                rows = pl.ds(36 * i + 30, 6)
-                acc[c, rows, :] = acc[c, rows, :] - e_high[c, pl.ds(6 * i, 6), :]
+        weight = step_row * STAGES[s][2]
+        for c, flux in enumerate(
+            face_flux(packed(wide_below.at[s]), packed(own_low.at[s]), 1)
+        ):
+            rows = pl.ds(c, PACK, stride=9)
+            own_low[s + 1, rows, :] = own_low[s + 1, rows, :] + weight * flux
+        for c, flux in enumerate(
+            face_flux(packed(own_high.at[s]), packed(wide_above.at[s]), 1)
+        ):
+            rows = pl.ds(c, PACK, stride=9)
+            own_high[s + 1, rows, :] = own_high[s + 1, rows, :] - weight * flux
 
     def length_edges(s):
         u_ref = states[s]
@@ -524,18 +542,16 @@
             for c in range(9):
                 acc[c, rows, :] = acc[c, rows, :] - flux[c]
 
-    def update(s, step):
+    def update(s, step, spans):
         first, own, factor = STAGES[s]
         weight = step * factor
-        for c in range(9):
-            rows = pl.ds(0, NODES)
-            new = own * states[s][c, rows, :] + weight * acc[c, rows, :]
-            if first:
-                new = new + first * u0[c, rows, :]
-            if s < 2:
+        for start, count in spans:
+            for c in range(9):
+                rows = pl.ds(start, count)
+                new = own * states[s][c, rows, :] + weight * acc[c, rows, :]
+                if first:
+                    new = new + first * u0[c, rows, :]
                 states[s + 1][c, rows, :] = new
-            else:
-                out_ref[c] = new
 
     def peak_copy(src, dst, which, step, peer):
         return pltpu.make_async_remote_copy(
@@ -547,41 +563,57 @@
             device_id_type=MESH,
         )
 
-    peak[...] = jnp.full((1, LANES), GLM_SPEED, jnp.float32)
-    send(0)
-    volume(0)
+    inner_rows = ((HALO, NODES - 2 * HALO),)
+    outer_rows = ((0, HALO), (NODES - HALO, HALO))
+
+    load_u.wait()
+    largest_speed()
+    gather(0)
+    for load in load_kinds:
+        load.wait()
+    low_wall = jnp.where(z == 0, wall_row(0), 3)
+    high_wall = wall_row(1)
+    neighbours = has_prev.astype(jnp.int32) + has_next.astype(jnp.int32)
+    pl.semaphore_wait(barrier, group - 1 + crowd - 1 + neighbours)
+    send_width(0)
 
     @pl.loop(1, group)
     def _(step):
         peak_copy(peak, peak_group, 0, step, group_peer(step)).start()
 
-    load_m.wait()
-    derivatives()
-    pltpu.make_async_copy(peak_group, peak_group, peak_recv.at[0]).wait()
-    pltpu.make_async_copy(peak_group, peak_group, peak_send.at[0]).wait()
-    peak[...] = jnp.maximum(peak[...], jnp.max(peak_group[...], axis=0))
-
-    @pl.loop(1, crowd)
-    def _(step):
-        peak_copy(peak, peak_all, 1, step, crowd_peer(step)).start()
-
-    inner_faces(0)
-    width_edges(0)
-    length_edges(0)
-    pltpu.make_async_copy(peak_all, peak_all, peak_recv.at[1]).wait()
-    fastest = jnp.max(jnp.maximum(peak[...], jnp.max(peak_all[...], axis=0)), axis=1, keepdims=True)
-    step_row = CFL_NUMBER / (11.0 * jnp.broadcast_to(fastest, (1, LANES)))
-    dt_ref[0, 0] = jnp.max(step_row)
-    update(0, step_row)
-
-    for s in (1, 2):
-        send(s)
+    step_row = None
+    for s in range(3):
+        send_length(s)
         volume(s)
+        if s == 0:
+            load_m.wait()
         derivatives()
-        inner_faces(s)
-        width_edges(s)
+        if s == 0:
+            pltpu.make_async_copy(peak_group, peak_group, peak_recv.at[0]).wait()
+            pltpu.make_async_copy(peak_group, peak_group, peak_send.at[0]).wait()
+            peak[...] = jnp.maximum(peak[...], jnp.max(peak_group[...], axis=0))
+
+            @pl.loop(1, crowd)
+            def _(step):
+                peak_copy(peak, peak_all, 1, step, crowd_peer(step)).start()
+
+        inner_faces(s, low_wall, high_wall)
+        if s:
+            update(s, step_row, inner_rows)
         length_edges(s)
-        update(s, step_row)
+        if s == 0:
+            pltpu.make_async_copy(peak_all, peak_all, peak_recv.at[1]).wait()
+            fastest = jnp.maximum(peak[...], jnp.max(peak_all[...], axis=0))
+            fastest = jnp.max(fastest, axis=1, keepdims=True)
+            step_row = CFL_NUMBER / (11.0 * jnp.broadcast_to(fastest, (1, LANES)))
+            dt_ref[0, 0] = jnp.max(step_row)
+            update(s, step_row, inner_rows)
+        update(s, step_row, outer_rows)
+        gather(s + 1)
+        width_edges(s, step_row)
+        if s < 2:
+            send_width(s + 1)
+        scatter(s + 1)
 
     pltpu.make_async_copy(peak_all, peak_all, peak_send.at[1]).wait()
     for s in range(3):
@@ -610,6 +642,7 @@
         state = pltpu.VMEM((9, PADDED, LANES), f32)
         halo = pltpu.VMEM((3, 9, HALO, LANES), f32)
         pack = pltpu.VMEM((3, 9 * PACK, LANES), f32)
+        own_pack = pltpu.VMEM((4, 9 * PACK, LANES), f32)
         trace = pltpu.VMEM((9, HALO, LANES), f32)
         flux = pltpu.VMEM((3 * PADDED, 9 * LANES), jnp.bfloat16)
         updated, step = pl.pallas_call(
@@ -618,9 +651,12 @@
                 jax.ShapeDtypeStruct((9, NODES, LANES), f32),
                 jax.ShapeDtypeStruct((1, 1), f32),
             ),
-            in_specs=[hbm, hbm, vmem, vmem, vmem],
+            in_specs=[hbm] * 5,
             out_specs=(vmem, pl.BlockSpec(memory_space=pltpu.SMEM)),
             scratch_shapes=[
+                pltpu.VMEM((2, LANES // EZ, EZ), jnp.int32),
+                pltpu.VMEM((2, 1, EZ), jnp.int32),
+                pltpu.VMEM((2, 1, LANES // EZ), jnp.int32),
                 state,
                 state,
                 state,
@@ -630,19 +666,17 @@
                 state,
                 halo,
                 halo,
-                pack,
-                pack,
+                own_pack,
+                own_pack,
                 pack,
                 pack,
                 trace,
                 trace,
                 trace,
-                trace,
-                trace,
                 pltpu.VMEM((1, LANES), f32),
-                pltpu.VMEM((group - 1, 1, LANES), f32),
-                pltpu.VMEM((crowd - 1, 1, LANES), f32),
-                pltpu.SemaphoreType.DMA((2,)),
+                pltpu.VMEM((max(group - 1, 1), 1, LANES), f32),
+                pltpu.VMEM((max(crowd - 1, 1), 1, LANES), f32),
+                pltpu.SemaphoreType.DMA((5,)),
                 pltpu.SemaphoreType.DMA((3, 4)),
                 pltpu.SemaphoreType.DMA((3, 4)),
                 pltpu.SemaphoreType.DMA((2,)),
@@ -652,11 +686,16 @@
                 collective_id=0, has_side_effects=True, vmem_limit_bytes=40 * 1024 * 1024
             ),
         )(
-            conserved.reshape(9, NODES, LANES),
-            jnp.asarray(matrix),
-            ends_kind,
-            sides_kind,
-            walls_kind,
+            *(
+                pltpu.with_memory_space_constraint(x, pltpu.HBM)
+                for x in (
+                    conserved.reshape(9, NODES, LANES),
+                    jnp.asarray(matrix),
+                    ends_kind,
+                    sides_kind,
+                    walls_kind,
+                )
+            )
         )
         return updated.reshape(conserved.shape), step.reshape(())
 

time: 48.8 us -> 42.4 us (0.87)
  the two profiles are of different devices: /device:TPU:27 before, /device:TPU:34 now
where the time goes in v2:
time: 42.4 us; the launch traced here: 42.3 us
  Pallas kernels  39 us (92%)
  between operations  2.33 us (5%)
  local copies, waits for them, and re-layouts  0.95 us (2%)
    pallas_call x1, Pallas kernels, on_device(): pl.pallas_call(functools.partial(kernel, nlen, nwid), out_shape=(jax.Shap...  39 us
    unnamed x1, local copies, waits for them, and re-layouts  0.95 us

profile of v2, /device:TPU:34, one launch (start us, length us, event | category | flops | bytes accessed | tf_op | source)
XLA Modules:
  0.0 42.3 jit_solution(8947712296877948359)
XLA Ops:
  0.6 39.0 %shard_map.68 = (f32[9,216,128]{2,1,0:T(8,128)S(1)}, f32[1,1]{1,0:T(1,128)}) custom-call(f32[9,216,128]{2,1,0:T(8,128)} %bitcast.4, bf16[2,224,672]{2,1,0:T(8,128)(2,1)} %constant.2.clone.mat_hbm, s32[2,4,32]{2,1,0:T(4,128)} %ends_hbm.1, s32[2,1,32]{2,1,0:T(1,128)} %sides_hbm.1, s32[2,1,4]{2,1,0:T(1,128)} %walls_hbm.1), custom_call_target="tpu_custom_call" | custom-call | tf_op jit(solution)/shard_map/pallas_call | solution.py:648
  39.6 1.0 %copy.11 = f32[9,6,6,6,1,128]{5,4,3,2,1,0:T(1,128)} copy(f32[9,6,6,6,1,128]{5,4,3,2,1,0:T(1,128)S(1)} %bitcast.3) | data formatting | bytes 1990656

commit v3 on v2

--- a/solution.py
+++ b/solution.py
@@ -183,8 +183,16 @@
     own_high,
     wide_below,
     wide_above,
+    acc_low,
+    acc_high,
+    ghost_low,
+    ghost_high,
+    e_low,
+    e_high,
     t_low,
     t_high,
+    a_low,
+    a_high,
     g_wide,
     peak,
     peak_group,
@@ -295,7 +303,7 @@
 
     def copy_left(s):
         return pltpu.make_async_remote_copy(
-            src_ref=own_low.at[s],
+            src_ref=own_low.at[0] if s == 0 else acc_low.at[s - 1],
             dst_ref=wide_above.at[s],
             send_sem=send_sem.at[s, 2],
             recv_sem=recv_sem.at[s, 2],
@@ -305,7 +313,7 @@
 
     def copy_right(s):
         return pltpu.make_async_remote_copy(
-            src_ref=own_high.at[s],
+            src_ref=own_high.at[0] if s == 0 else acc_high.at[s - 1],
             dst_ref=wide_below.at[s],
             send_sem=send_sem.at[s, 3],
             recv_sem=recv_sem.at[s, 3],
@@ -338,19 +346,24 @@
         def _():
             copy_next(s).start()
 
-    def gather(s):
-        u = states[s]
+    def traces(ref, low, high):
         for c in range(9):
             for i in range(6):
-                t_low[c, pl.ds(6 * i, 6), :] = u[c, pl.ds(36 * i, 6), :]
-                t_high[c, pl.ds(6 * i, 6), :] = u[c, pl.ds(36 * i + 30, 6), :]
-        for ref, dest, first in ((t_low, own_low, 0), (t_high, own_high, wide - 1)):
-            for c in range(9):
-                whole = None
-                for q in range(wide):
-                    piece = roll(ref[c, pl.ds(q, PACK, stride=4), :], EZ * (q - first))
-                    whole = piece if q == 0 else jnp.where(y == q, piece, whole)
-                dest[s, pl.ds(c, PACK, stride=9), :] = whole
+                low[c, pl.ds(6 * i, 6), :] = ref[c, pl.ds(36 * i, 6), :]
+                high[c, pl.ds(6 * i, 6), :] = ref[c, pl.ds(36 * i + 30, 6), :]
+
+    def pack(ref, dest, slot, first):
+        for c in range(9):
+            whole = None
+            for q in range(wide):
+                piece = roll(ref[c, pl.ds(q, PACK, stride=4), :], EZ * (q - first))
+                whole = piece if q == 0 else jnp.where(y == q, piece, whole)
+            dest[slot, pl.ds(c, PACK, stride=9), :] = whole
+
+    def pack_width(s):
+        traces(acc, a_low, a_high)
+        pack(a_low, acc_low, s, 0)
+        pack(a_high, acc_high, s, wide - 1)
 
     def scatter(s):
         u = states[s]
@@ -425,8 +438,10 @@
         top = lax.fori_loop(0, NODES // 8, body, start, unroll=3)
         peak[...] = jnp.max(top, axis=0, keepdims=True)
 
-    def derivatives():
+    def derivatives(midway=None):
         for first in range(0, 9, 2):
+            if first == 4 and midway is not None:
+                midway()
             count = min(2, 9 - first)
             span = pl.ds(first * LANES, count * LANES)
             high = fhi[:, span]
@@ -467,38 +482,52 @@
                 rows = pl.ds(36 * i + 30, 6)
                 acc[c, rows, :] = acc[c, rows, :] - jnp.where(y < wide - 1, roll(flux, -EZ), 0.0)
 
-    def width_edges(s, step_row):
-        @pl.when(has_left)
-        def _():
-            copy_right(s).wait_recv()
-
-        @pl.when(has_right)
-        def _():
-            copy_left(s).wait_recv()
-
-        @pl.when(jnp.logical_not(has_left))
-        def _():
-            outer = with_outer(None, packed(own_low.at[s]), tiled(sides_ref[0]), 1, -1.0)
+    def advance(s, step, start, current, change):
+        first, own, factor = STAGES[s]
+        new = own * current + (step * factor) * change
+        return new + first * start if first else new
+
+    def width_edges(s, step):
+        sides = (
+            (has_left, copy_right, wide_below, ghost_low, e_low, -1.0, own_low, 0),
+            (has_right, copy_left, wide_above, ghost_high, e_high, 1.0, own_high, 1),
+        )
+        for have, copy, received, ghost, edge, sign, own, side in sides:
+
+            @pl.when(have)
+            def _(copy=copy, received=received, ghost=ghost, edge=edge, sign=sign):
+                copy(s).wait_recv()
+                for c in range(9):
+                    rows = pl.ds(c, PACK, stride=9)
+                    new = received[s, rows, :]
+                    if s:
+                        change = new + sign * edge[s - 1, rows, :]
+                        old = ghost[s - 1, rows, :]
+                        new = advance(s - 1, step, ghost[0, rows, :], old, change)
+                    ghost[s, rows, :] = new
+
+            @pl.when(jnp.logical_not(have))
+            def _(ghost=ghost, own=own, side=side, sign=sign):
+                outer = with_outer(None, packed(own.at[s]), tiled(sides_ref[side]), 1, sign)
+                for c in range(9):
+                    ghost[s, pl.ds(c, PACK, stride=9), :] = outer[c]
+
+        low = face_flux(packed(ghost_low.at[s]), packed(own_low.at[s]), 1)
+        high = face_flux(packed(own_high.at[s]), packed(ghost_high.at[s]), 1)
+        for fluxes, edge, own, change, sign in (
+            (low, e_low, own_low, acc_low, 1.0),
+            (high, e_high, own_high, acc_high, -1.0),
+        ):
             for c in range(9):
-                wide_below[s, pl.ds(c, PACK, stride=9), :] = outer[c]
-
-        @pl.when(jnp.logical_not(has_right))
-        def _():
-            outer = with_outer(None, packed(own_high.at[s]), tiled(sides_ref[1]), 1, 1.0)
-            for c in range(9):
-                wide_above[s, pl.ds(c, PACK, stride=9), :] = outer[c]
-
-        weight = step_row * STAGES[s][2]
-        for c, flux in enumerate(
-            face_flux(packed(wide_below.at[s]), packed(own_low.at[s]), 1)
-        ):
-            rows = pl.ds(c, PACK, stride=9)
-            own_low[s + 1, rows, :] = own_low[s + 1, rows, :] + weight * flux
-        for c, flux in enumerate(
-            face_flux(packed(own_high.at[s]), packed(wide_above.at[s]), 1)
-        ):
-            rows = pl.ds(c, PACK, stride=9)
-            own_high[s + 1, rows, :] = own_high[s + 1, rows, :] - weight * flux
+                rows = pl.ds(c, PACK, stride=9)
+                edge[s, rows, :] = fluxes[c]
+                own[s + 1, rows, :] = advance(
+                    s,
+                    step,
+                    own[0, rows, :],
+                    own[s, rows, :],
+                    change[s, rows, :] + sign * fluxes[c],
+                )
 
     def length_edges(s):
         u_ref = states[s]
@@ -566,9 +595,20 @@
     inner_rows = ((HALO, NODES - 2 * HALO),)
     outer_rows = ((0, HALO), (NODES - HALO, HALO))
 
+    def second_round():
+        pltpu.make_async_copy(peak_group, peak_group, peak_recv.at[0]).wait()
+        pltpu.make_async_copy(peak_group, peak_group, peak_send.at[0]).wait()
+        peak[...] = jnp.maximum(peak[...], jnp.max(peak_group[...], axis=0))
+
+        @pl.loop(1, crowd)
+        def _(step):
+            peak_copy(peak, peak_all, 1, step, crowd_peer(step)).start()
+
     load_u.wait()
     largest_speed()
-    gather(0)
+    traces(u0, t_low, t_high)
+    pack(t_low, own_low, 0, 0)
+    pack(t_high, own_high, 0, wide - 1)
     for load in load_kinds:
         load.wait()
     low_wall = jnp.where(z == 0, wall_row(0), 3)
@@ -587,20 +627,14 @@
         volume(s)
         if s == 0:
             load_m.wait()
-        derivatives()
-        if s == 0:
-            pltpu.make_async_copy(peak_group, peak_group, peak_recv.at[0]).wait()
-            pltpu.make_async_copy(peak_group, peak_group, peak_send.at[0]).wait()
-            peak[...] = jnp.maximum(peak[...], jnp.max(peak_group[...], axis=0))
-
-            @pl.loop(1, crowd)
-            def _(step):
-                peak_copy(peak, peak_all, 1, step, crowd_peer(step)).start()
-
+        derivatives(second_round if s == 0 else None)
         inner_faces(s, low_wall, high_wall)
         if s:
             update(s, step_row, inner_rows)
         length_edges(s)
+        pack_width(s)
+        if s < 2:
+            send_width(s + 1)
         if s == 0:
             pltpu.make_async_copy(peak_all, peak_all, peak_recv.at[1]).wait()
             fastest = jnp.maximum(peak[...], jnp.max(peak_all[...], axis=0))
@@ -609,10 +643,8 @@
             dt_ref[0, 0] = jnp.max(step_row)
             update(s, step_row, inner_rows)
         update(s, step_row, outer_rows)
-        gather(s + 1)
+        traces(states[s + 1], t_low, t_high)
         width_edges(s, step_row)
-        if s < 2:
-            send_width(s + 1)
         scatter(s + 1)
 
     pltpu.make_async_copy(peak_all, peak_all, peak_send.at[1]).wait()
@@ -670,6 +702,14 @@
                 own_pack,
                 pack,
                 pack,
+                pack,
+                pack,
+                pack,
+                pack,
+                pack,
+                pack,
+                trace,
+                trace,
                 trace,
                 trace,
                 trace,

time: 42.4 us -> 38.9 us (0.917)
  the two profiles are of different devices: /device:TPU:34 before, /device:TPU:27 now
where the time goes in v3:
time: 38.9 us; the launch traced here: 38.7 us
  Pallas kernels  35.5 us (91%)
  between operations  2.33 us (6%)
  local copies, waits for them, and re-layouts  0.95 us (2%)
    pallas_call x1, Pallas kernels, on_device(): pl.pallas_call(functools.partial(kernel, nlen, nwid), out_shape=(jax.Shap...  35.5 us
    unnamed x1, local copies, waits for them, and re-layouts  0.95 us

profile of v3, /device:TPU:27, one launch (start us, length us, event | category | flops | bytes accessed | tf_op | source)
XLA Modules:
  0.0 38.7 jit_solution(5816650259270408407)
XLA Ops:
  0.6 35.5 %shard_map.68 = (f32[9,216,128]{2,1,0:T(8,128)S(1)}, f32[1,1]{1,0:T(1,128)}) custom-call(f32[9,216,128]{2,1,0:T(8,128)} %bitcast.4, bf16[2,224,672]{2,1,0:T(8,128)(2,1)} %constant.2.clone.mat_hbm, s32[2,4,32]{2,1,0:T(4,128)} %ends_hbm.1, s32[2,1,32]{2,1,0:T(1,128)} %sides_hbm.1, s32[2,1,4]{2,1,0:T(1,128)} %walls_hbm.1), custom_call_target="tpu_custom_call" | custom-call | tf_op jit(solution)/shard_map/pallas_call | solution.py:680
  36.1 1.0 %copy.11 = f32[9,6,6,6,1,128]{5,4,3,2,1,0:T(1,128)} copy(f32[9,6,6,6,1,128]{5,4,3,2,1,0:T(1,128)S(1)} %bitcast.3) | data formatting | bytes 1990656

commit v4 on v3

--- a/solution.py
+++ b/solution.py
@@ -71,6 +71,11 @@
     high = whole.astype(jnp.bfloat16)
     low = (whole - high.astype(np.float32)).astype(jnp.bfloat16)
     return np.stack([high, low])
+
+
+def peak_rounds(nlen, nwid):
+    near = min(8, nlen)
+    return near, nwid // 2, nlen // near * 2
 
 
 def root(x):
@@ -195,8 +200,9 @@
     a_high,
     g_wide,
     peak,
-    peak_group,
-    peak_all,
+    peaks0,
+    peaks1,
+    peaks2,
     load_sem,
     send_sem,
     recv_sem,
@@ -205,11 +211,11 @@
 ):
     li = lax.axis_index("len")
     wi = lax.axis_index("wid")
-    group = max(nlen // 2, 1)
-    blocks = nlen // group
-    crowd = blocks * nwid
+    rounds = peak_rounds(nlen, nwid)
+    near, rows_of_chips, columns = rounds
     lanes = lax.broadcasted_iota(jnp.int32, (1, LANES), 1)
     states = (u0, u1, u2, out_ref)
+    peaks = (peaks0, peaks1, peaks2)
 
     load_u = pltpu.make_async_copy(u_hbm, u0.at[:, pl.ds(0, NODES), :], load_sem.at[0])
     load_m = pltpu.make_async_copy(mat_hbm, mat, load_sem.at[1])
@@ -224,42 +230,40 @@
         load.start()
     load_m.start()
 
-    in_group = lax.rem(li, group)
-    block = li // group
-    base = block * group
-    in_crowd = block * nwid + wi
-
-    def group_peer(step):
-        return (base + lax.rem(in_group + step, group), wi)
-
-    def crowd_peer(step):
-        other = lax.rem(in_crowd + step, crowd)
-        return ((other // nwid) * group + in_group, lax.rem(other, nwid))
+    in_near, block = lax.rem(li, near), li // near
+    in_column, row = lax.rem(wi, 2), wi // 2
+    in_columns = block * 2 + in_column
+
+    def peer(which, step):
+        if which == 0:
+            return (block * near + lax.rem(in_near + step, near), wi)
+        if which == 1:
+            return (li, lax.rem(row + step, rows_of_chips) * 2 + in_column)
+        other = lax.rem(in_columns + step, columns)
+        return ((other // 2) * near + in_near, row * 2 + lax.rem(other, 2))
 
     barrier = pltpu.get_barrier_semaphore()
 
-    def greet(peer):
-        pl.semaphore_signal(barrier, inc=1, device_id=peer, device_id_type=MESH)
+    def greet(device):
+        pl.semaphore_signal(barrier, inc=1, device_id=device, device_id_type=MESH)
 
     has_prev, has_next = li > 0, li < nlen - 1
     has_left, has_right = wi > 0, wi < nwid - 1
 
-    for step in range(1, crowd // 2 + 1):
-        greet(crowd_peer(step))
-        if step < crowd - step:
-            greet(crowd_peer(crowd - step))
-
-    @pl.when(has_prev)
-    def _():
-        greet((li - 1, wi))
-
-    @pl.when(has_next)
-    def _():
-        greet((li + 1, wi))
-
-    @pl.loop(1, group)
-    def _(step):
-        greet(group_peer(step))
+    for have, device in (
+        (has_left, (li, wi - 1)),
+        (has_right, (li, wi + 1)),
+        (has_prev, (li - 1, wi)),
+        (has_next, (li + 1, wi)),
+    ):
+
+        @pl.when(have)
+        def _(device=device):
+            greet(device)
+
+    for which in (2, 1, 0):
+        for step in range(1, rounds[which]):
+            greet(peer(which, step))
 
     for ref in states[:3]:
         for c in range(9):
@@ -436,7 +440,7 @@
 
         start = jnp.full((8, LANES), GLM_SPEED, jnp.float32)
         top = lax.fori_loop(0, NODES // 8, body, start, unroll=3)
-        peak[...] = jnp.max(top, axis=0, keepdims=True)
+        peak[0] = jnp.max(top, axis=0, keepdims=True)
 
     def derivatives(midway=None):
         for first in range(0, 9, 2):
@@ -582,52 +586,57 @@
                     new = new + first * u0[c, rows, :]
                 states[s + 1][c, rows, :] = new
 
-    def peak_copy(src, dst, which, step, peer):
-        return pltpu.make_async_remote_copy(
-            src_ref=src,
-            dst_ref=dst.at[step - 1],
-            send_sem=peak_send.at[which],
-            recv_sem=peak_recv.at[which],
-            device_id=peer,
-            device_id_type=MESH,
-        )
+    def peak_send_round(which):
+        for step in range(1, rounds[which]):
+            pltpu.make_async_remote_copy(
+                src_ref=peak.at[which],
+                dst_ref=peaks[which].at[step - 1],
+                send_sem=peak_send.at[which],
+                recv_sem=peak_recv.at[which],
+                device_id=peer(which, step),
+                device_id_type=MESH,
+            ).start()
+
+    def peak_wait_round(which):
+        top = peak[which]
+        if rounds[which] > 1:
+            got = peaks[which]
+            pltpu.make_async_copy(got, got, peak_recv.at[which]).wait()
+            top = jnp.maximum(top, jnp.max(got[...], axis=0))
+        peak[which + 1] = top
 
     inner_rows = ((HALO, NODES - 2 * HALO),)
     outer_rows = ((0, HALO), (NODES - HALO, HALO))
 
-    def second_round():
-        pltpu.make_async_copy(peak_group, peak_group, peak_recv.at[0]).wait()
-        pltpu.make_async_copy(peak_group, peak_group, peak_send.at[0]).wait()
-        peak[...] = jnp.maximum(peak[...], jnp.max(peak_group[...], axis=0))
-
-        @pl.loop(1, crowd)
-        def _(step):
-            peak_copy(peak, peak_all, 1, step, crowd_peer(step)).start()
+    def third_round():
+        peak_wait_round(1)
+        peak_send_round(2)
 
     load_u.wait()
     largest_speed()
+    neighbours = sum(have.astype(jnp.int32) for have in (has_prev, has_next, has_left, has_right))
+    pl.semaphore_wait(barrier, sum(rounds) - 3 + neighbours)
+    peak_send_round(0)
     traces(u0, t_low, t_high)
     pack(t_low, own_low, 0, 0)
     pack(t_high, own_high, 0, wide - 1)
+    send_width(0)
     for load in load_kinds:
         load.wait()
     low_wall = jnp.where(z == 0, wall_row(0), 3)
     high_wall = wall_row(1)
-    neighbours = has_prev.astype(jnp.int32) + has_next.astype(jnp.int32)
-    pl.semaphore_wait(barrier, group - 1 + crowd - 1 + neighbours)
-    send_width(0)
-
-    @pl.loop(1, group)
-    def _(step):
-        peak_copy(peak, peak_group, 0, step, group_peer(step)).start()
 
     step_row = None
     for s in range(3):
-        send_length(s)
+        if s:
+            send_length(s)
         volume(s)
         if s == 0:
+            peak_wait_round(0)
+            peak_send_round(1)
+            send_length(0)
             load_m.wait()
-        derivatives(second_round if s == 0 else None)
+        derivatives(third_round if s == 0 else None)
         inner_faces(s, low_wall, high_wall)
         if s:
             update(s, step_row, inner_rows)
@@ -636,9 +645,8 @@
         if s < 2:
             send_width(s + 1)
         if s == 0:
-            pltpu.make_async_copy(peak_all, peak_all, peak_recv.at[1]).wait()
-            fastest = jnp.maximum(peak[...], jnp.max(peak_all[...], axis=0))
-            fastest = jnp.max(fastest, axis=1, keepdims=True)
+            peak_wait_round(2)
+            fastest = jnp.max(peak[3], axis=1, keepdims=True)
             step_row = CFL_NUMBER / (11.0 * jnp.broadcast_to(fastest, (1, LANES)))
             dt_ref[0, 0] = jnp.max(step_row)
             update(s, step_row, inner_rows)
@@ -647,7 +655,9 @@
         width_edges(s, step_row)
         scatter(s + 1)
 
-    pltpu.make_async_copy(peak_all, peak_all, peak_send.at[1]).wait()
+    for which in range(3):
+        if rounds[which] > 1:
+            pltpu.make_async_copy(peaks[which], peaks[which], peak_send.at[which]).wait()
     for s in range(3):
         for have, copy in (
             (has_prev, copy_prev),
@@ -663,8 +673,7 @@
 
 def solution(mesh):
     nlen, nwid = mesh.shape["len"], mesh.shape["wid"]
-    group = max(nlen // 2, 1)
-    crowd = nlen // group * nwid
+    rounds = peak_rounds(nlen, nwid)
     matrix = volume_matrix()
 
     def on_device(conserved, ends_kind, sides_kind, walls_kind):
@@ -713,14 +722,13 @@
                 trace,
                 trace,
                 trace,
-                pltpu.VMEM((1, LANES), f32),
-                pltpu.VMEM((max(group - 1, 1), 1, LANES), f32),
-                pltpu.VMEM((max(crowd - 1, 1), 1, LANES), f32),
+                pltpu.VMEM((4, 1, LANES), f32),
+                *(pltpu.VMEM((max(size - 1, 1), 1, LANES), f32) for size in rounds),
                 pltpu.SemaphoreType.DMA((5,)),
                 pltpu.SemaphoreType.DMA((3, 4)),
                 pltpu.SemaphoreType.DMA((3, 4)),
-                pltpu.SemaphoreType.DMA((2,)),
-                pltpu.SemaphoreType.DMA((2,)),
+                pltpu.SemaphoreType.DMA((3,)),
+                pltpu.SemaphoreType.DMA((3,)),
             ],
             compiler_params=pltpu.CompilerParams(
                 collective_id=0, has_side_effects=True, vmem_limit_bytes=40 * 1024 * 1024

time: 38.9 us -> 38 us (0.977)
  Pallas kernels: 35.5 us -> 34.2 us
    pallas_call x1, Pallas kernels: 35.5 us -> 34.2 us  [on_device(): pl.pallas_call(functools.partial(kernel, nlen, nwid), out_shape=(jax.Shap...]
where the time goes in v4:
time: 38 us; the launch traced here: 37.5 us
  Pallas kernels  34.2 us (90%)
  between operations  2.33 us (6%)
  local copies, waits for them, and re-layouts  0.95 us (2%)
    pallas_call x1, Pallas kernels, on_device(): pl.pallas_call(functools.partial(kernel, nlen, nwid), out_shape=(jax.Shap...  34.2 us
    unnamed x1, local copies, waits for them, and re-layouts  0.95 us

profile of v4, /device:TPU:27, one launch (start us, length us, event | category | flops | bytes accessed | tf_op | source)
XLA Modules:
  0.0 37.5 jit_solution(17059442754862551838)
XLA Ops:
  0.6 34.2 %shard_map.68 = (f32[9,216,128]{2,1,0:T(8,128)S(1)}, f32[1,1]{1,0:T(1,128)}) custom-call(f32[9,216,128]{2,1,0:T(8,128)} %bitcast.4, bf16[2,224,672]{2,1,0:T(8,128)(2,1)} %constant.2.clone.mat_hbm, s32[2,4,32]{2,1,0:T(4,128)} %ends_hbm.1, s32[2,1,32]{2,1,0:T(1,128)} %sides_hbm.1, s32[2,1,4]{2,1,0:T(1,128)} %walls_hbm.1), custom_call_target="tpu_custom_call" | custom-call | tf_op jit(solution)/shard_map/pallas_call | solution.py:689
  34.9 1.0 %copy.11 = f32[9,6,6,6,1,128]{5,4,3,2,1,0:T(1,128)} copy(f32[9,6,6,6,1,128]{5,4,3,2,1,0:T(1,128)S(1)} %bitcast.3) | data formatting | bytes 1990656

commit v5 on v4

--- a/solution.py
+++ b/solution.py
@@ -181,7 +181,8 @@
     mat,
     fhi,
     flo,
-    acc,
+    acc0,
+    acc1,
     above,
     below,
     own_low,
@@ -215,6 +216,7 @@
     near, rows_of_chips, columns = rounds
     lanes = lax.broadcasted_iota(jnp.int32, (1, LANES), 1)
     states = (u0, u1, u2, out_ref)
+    accs = (acc0, acc1, acc1)
     peaks = (peaks0, peaks1, peaks2)
 
     load_u = pltpu.make_async_copy(u_hbm, u0.at[:, pl.ds(0, NODES), :], load_sem.at[0])
@@ -287,8 +289,8 @@
 
     def copy_prev(s):
         return pltpu.make_async_remote_copy(
-            src_ref=states[s].at[:, pl.ds(0, HALO), :],
-            dst_ref=above.at[s],
+            src_ref=(u0, acc0, u2)[s].at[:, pl.ds(0, HALO), :],
+            dst_ref=above.at[(0, 3, 2)[s]],
             send_sem=send_sem.at[s, 0],
             recv_sem=recv_sem.at[s, 0],
             device_id=(li - 1, wi),
@@ -297,8 +299,8 @@
 
     def copy_next(s):
         return pltpu.make_async_remote_copy(
-            src_ref=states[s].at[:, pl.ds(NODES - HALO, HALO), :],
-            dst_ref=below.at[s],
+            src_ref=(u0, acc0, u2)[s].at[:, pl.ds(NODES - HALO, HALO), :],
+            dst_ref=below.at[(0, 3, 2)[s]],
             send_sem=send_sem.at[s, 1],
             recv_sem=recv_sem.at[s, 1],
             device_id=(li + 1, wi),
@@ -365,15 +367,14 @@
             dest[slot, pl.ds(c, PACK, stride=9), :] = whole
 
     def pack_width(s):
-        traces(acc, a_low, a_high)
+        traces(accs[s], a_low, a_high)
         pack(a_low, acc_low, s, 0)
         pack(a_high, acc_high, s, wide - 1)
 
-    def scatter(s):
-        u = states[s]
-        for ref, src, first in ((t_low, own_low, 0), (t_high, own_high, wide - 1)):
-            for c in range(9):
-                new = src[s, pl.ds(c, PACK, stride=9), :]
+    def scatter(slot, low, high, target):
+        for ref, src, first in ((low, own_low, 0), (high, own_high, wide - 1)):
+            for c in range(9):
+                new = src[slot, pl.ds(c, PACK, stride=9), :]
                 for q in range(wide):
                     rows = pl.ds(q, PACK, stride=4)
                     ref[c, rows, :] = jnp.where(
@@ -381,8 +382,8 @@
                     )
         for c in range(9):
             for i in range(6):
-                u[c, pl.ds(36 * i, 6), :] = t_low[c, pl.ds(6 * i, 6), :]
-                u[c, pl.ds(36 * i + 30, 6), :] = t_high[c, pl.ds(6 * i, 6), :]
+                target[c, pl.ds(36 * i, 6), :] = low[c, pl.ds(6 * i, 6), :]
+                target[c, pl.ds(36 * i + 30, 6), :] = high[c, pl.ds(6 * i, 6), :]
 
     def volume(s):
         u_ref = states[s]
@@ -442,7 +443,8 @@
         top = lax.fori_loop(0, NODES // 8, body, start, unroll=3)
         peak[0] = jnp.max(top, axis=0, keepdims=True)
 
-    def derivatives(midway=None):
+    def derivatives(s, midway=None):
+        acc = accs[s]
         for first in range(0, 9, 2):
             if first == 4 and midway is not None:
                 midway()
@@ -456,6 +458,7 @@
                 acc[first + c] = result[:, c * LANES : (c + 1) * LANES]
 
     def inner_faces(s, low_wall, high_wall):
+        acc = accs[s]
         u_ref = states[s]
         for first, count in CHUNKS:
             low_rows = pl.ds(6 * first, count, stride=6)
@@ -525,26 +528,40 @@
             for c in range(9):
                 rows = pl.ds(c, PACK, stride=9)
                 edge[s, rows, :] = fluxes[c]
-                own[s + 1, rows, :] = advance(
-                    s,
-                    step,
-                    own[0, rows, :],
-                    own[s, rows, :],
-                    change[s, rows, :] + sign * fluxes[c],
-                )
-
-    def length_edges(s):
+                whole = change[s, rows, :] + sign * fluxes[c]
+                if s != 1:
+                    own[3, rows, :] = whole
+                else:
+                    own[s + 1, rows, :] = advance(
+                        s, step, own[0, rows, :], own[s, rows, :], whole
+                    )
+
+    def first_width(step):
+        for own in (own_low, own_high):
+            for c in range(9):
+                rows = pl.ds(c, PACK, stride=9)
+                start = own[0, rows, :]
+                own[1, rows, :] = advance(0, step, start, start, own[3, rows, :])
+
+    def length_edges(s, step):
         u_ref = states[s]
+        acc = accs[s]
         top = NODES - FACE
         skip = HALO - FACE
 
         @pl.when(has_prev)
         def _():
             copy_next(s).wait_recv()
+            if s == 1:
+                for c in range(9):
+                    below[1, c] = advance(0, step, below[0, c], below[0, c], below[3, c])
 
         @pl.when(has_next)
         def _():
             copy_prev(s).wait_recv()
+            if s == 1:
+                for c in range(9):
+                    above[1, c] = advance(0, step, above[0, c], above[0, c], above[3, c])
 
         @pl.when(jnp.logical_not(has_prev))
         def _():
@@ -581,7 +598,7 @@
         for start, count in spans:
             for c in range(9):
                 rows = pl.ds(start, count)
-                new = own * states[s][c, rows, :] + weight * acc[c, rows, :]
+                new = own * states[s][c, rows, :] + weight * accs[s][c, rows, :]
                 if first:
                     new = new + first * u0[c, rows, :]
                 states[s + 1][c, rows, :] = new
@@ -628,32 +645,46 @@
 
     step_row = None
     for s in range(3):
-        if s:
-            send_length(s)
+        if s == 2:
+            send_length(2)
         volume(s)
         if s == 0:
             peak_wait_round(0)
             peak_send_round(1)
             send_length(0)
             load_m.wait()
-        derivatives(third_round if s == 0 else None)
+        derivatives(s, third_round if s == 0 else None)
         inner_faces(s, low_wall, high_wall)
+        if s == 2:
+            pack_width(2)
+            width_edges(2, step_row)
+            scatter(3, a_low, a_high, acc1)
+            update(2, step_row, inner_rows)
+            length_edges(2, step_row)
+            update(2, step_row, outer_rows)
+            break
         if s:
             update(s, step_row, inner_rows)
-        length_edges(s)
+        length_edges(s, step_row)
         pack_width(s)
-        if s < 2:
-            send_width(s + 1)
+        send_width(s + 1)
         if s == 0:
+            width_edges(0, None)
+            scatter(3, a_low, a_high, acc0)
+            send_length(1)
             peak_wait_round(2)
             fastest = jnp.max(peak[3], axis=1, keepdims=True)
             step_row = CFL_NUMBER / (11.0 * jnp.broadcast_to(fastest, (1, LANES)))
             dt_ref[0, 0] = jnp.max(step_row)
-            update(s, step_row, inner_rows)
-        update(s, step_row, outer_rows)
-        traces(states[s + 1], t_low, t_high)
-        width_edges(s, step_row)
-        scatter(s + 1)
+            update(0, step_row, inner_rows)
+            update(0, step_row, outer_rows)
+            traces(states[1], t_low, t_high)
+            first_width(step_row)
+        else:
+            update(s, step_row, outer_rows)
+            traces(states[s + 1], t_low, t_high)
+            width_edges(s, step_row)
+            scatter(s + 1, t_low, t_high, states[s + 1])
 
     for which in range(3):
         if rounds[which] > 1:
@@ -681,7 +712,7 @@
         vmem = pl.BlockSpec(memory_space=pltpu.VMEM)
         hbm = pl.BlockSpec(memory_space=pl.ANY)
         state = pltpu.VMEM((9, PADDED, LANES), f32)
-        halo = pltpu.VMEM((3, 9, HALO, LANES), f32)
+        halo = pltpu.VMEM((4, 9, HALO, LANES), f32)
         pack = pltpu.VMEM((3, 9 * PACK, LANES), f32)
         own_pack = pltpu.VMEM((4, 9 * PACK, LANES), f32)
         trace = pltpu.VMEM((9, HALO, LANES), f32)
@@ -704,6 +735,7 @@
                 pltpu.VMEM((2, PADDED, 3 * PADDED), jnp.bfloat16),
                 flux,
                 flux,
+                state,
                 state,
                 halo,
                 halo,

time: 38 us -> 37.2 us (0.979); the launches traced: 37.5 us -> 37.1 us
  Pallas kernels: 34.2 us -> 33.8 us
where the time goes in v5:
time: 37.2 us; the launch traced here: 37.1 us
  Pallas kernels  33.8 us (91%)
  between operations  2.33 us (6%)
  local copies, waits for them, and re-layouts  0.95 us (3%)
    pallas_call x1, Pallas kernels, on_device(): pl.pallas_call(functools.partial(kernel, nlen, nwid), out_shape=(jax.Shap...  33.8 us
    unnamed x1, local copies, waits for them, and re-layouts  0.95 us

profile of v5, /device:TPU:27, one launch (start us, length us, event | category | flops | bytes accessed | tf_op | source)
XLA Modules:
  0.0 37.1 jit_solution(659877148655616556)
XLA Ops:
  0.6 33.8 %shard_map.68 = (f32[9,216,128]{2,1,0:T(8,128)S(1)}, f32[1,1]{1,0:T(1,128)}) custom-call(f32[9,216,128]{2,1,0:T(8,128)} %bitcast.4, bf16[2,224,672]{2,1,0:T(8,128)(2,1)} %constant.2.clone.mat_hbm, s32[2,4,32]{2,1,0:T(4,128)} %ends_hbm.1, s32[2,1,32]{2,1,0:T(1,128)} %sides_hbm.1, s32[2,1,4]{2,1,0:T(1,128)} %walls_hbm.1), custom_call_target="tpu_custom_call" | custom-call | tf_op jit(solution)/shard_map/pallas_call | solution.py:720
  34.5 1.0 %copy.11 = f32[9,6,6,6,1,128]{5,4,3,2,1,0:T(1,128)} copy(f32[9,6,6,6,1,128]{5,4,3,2,1,0:T(1,128)S(1)} %bitcast.3) | data formatting | bytes 1990656

commit v6 on v5

--- a/solution.py
+++ b/solution.py
@@ -24,6 +24,7 @@
 BRAKE_FIELD = 1.0
 CFL_NUMBER = 0.1
 LIFT = 30.0
+ORDER = (1, 2, 0)
 
 STAGES = ((0.0, 1.0, 1.0), (0.75, 0.25, 0.25), (1.0 / 3.0, 2.0 / 3.0, 2.0 / 3.0))
 
@@ -73,9 +74,13 @@
     return np.stack([high, low])
 
 
-def peak_rounds(nlen, nwid):
+def round_sizes(nlen, nwid):
     near = min(8, nlen)
     return near, nwid // 2, nlen // near * 2
+
+
+def peak_rounds(nlen, nwid):
+    return tuple(round_sizes(nlen, nwid)[n] for n in ORDER)
 
 
 def root(x):
@@ -213,7 +218,7 @@
     li = lax.axis_index("len")
     wi = lax.axis_index("wid")
     rounds = peak_rounds(nlen, nwid)
-    near, rows_of_chips, columns = rounds
+    near, rows_of_chips, columns = round_sizes(nlen, nwid)
     lanes = lax.broadcasted_iota(jnp.int32, (1, LANES), 1)
     states = (u0, u1, u2, out_ref)
     accs = (acc0, acc1, acc1)
@@ -237,6 +242,7 @@
     in_columns = block * 2 + in_column
 
     def peer(which, step):
+        which = ORDER[which]
         if which == 0:
             return (block * near + lax.rem(in_near + step, near), wi)
         if which == 1:

time: 37.2 us -> 36.7 us (0.987); the launches traced: 37.1 us -> 36.2 us
  Pallas kernels: 33.8 us -> 32.9 us
    pallas_call x1, Pallas kernels: 33.8 us -> 32.9 us  [on_device(): pl.pallas_call(functools.partial(kernel, nlen, nwid), out_shape=(jax.Shap...]
where the time goes in v6:
time: 36.7 us; the launch traced here: 36.2 us
  Pallas kernels  32.9 us (90%)
  between operations  2.33 us (6%)
  local copies, waits for them, and re-layouts  0.95 us (3%)
    pallas_call x1, Pallas kernels, on_device(): pl.pallas_call(functools.partial(kernel, nlen, nwid), out_shape=(jax.Shap...  32.9 us
    unnamed x1, local copies, waits for them, and re-layouts  0.95 us

profile of v6, /device:TPU:27, one launch (start us, length us, event | category | flops | bytes accessed | tf_op | source)
XLA Modules:
  0.0 36.2 jit_solution(12912270409699116725)
XLA Ops:
  0.6 32.9 %shard_map.68 = (f32[9,216,128]{2,1,0:T(8,128)S(1)}, f32[1,1]{1,0:T(1,128)}) custom-call(f32[9,216,128]{2,1,0:T(8,128)} %bitcast.4, bf16[2,224,672]{2,1,0:T(8,128)(2,1)} %constant.2.clone.mat_hbm, s32[2,4,32]{2,1,0:T(4,128)} %ends_hbm.1, s32[2,1,32]{2,1,0:T(1,128)} %sides_hbm.1, s32[2,1,4]{2,1,0:T(1,128)} %walls_hbm.1), custom_call_target="tpu_custom_call" | custom-call | tf_op jit(solution)/shard_map/pallas_call | solution.py:726
  33.5 1.0 %copy.11 = f32[9,6,6,6,1,128]{5,4,3,2,1,0:T(1,128)} copy(f32[9,6,6,6,1,128]{5,4,3,2,1,0:T(1,128)S(1)} %bitcast.3) | data formatting | bytes 1990656
